TPU v7x, 128 devices: a whole 4x4x4 slice. The times are simulated.
128 devices in a mesh: ctx: 16 (over z_hi, x, core), tp: 8 (over y, z_lo).
Axes of the slice: x: 4, y: 4, z: 4 (z_hi: 2, z_lo: 2; z = z_hi * 2 + z_lo), core: 2. Of those that a mesh axis runs over, the one named last changes fastest.
Arguments:
- outer_gate: bfloat16 [8192, 8192], P('ctx', 'tp'), may hold values from -6 to 6
- inner_gate: bfloat16 [8192, 8192], P('ctx', 'tp'), may hold values from -6 to 6
- signal: bfloat16 [8192, 8192], P('ctx', 'tp'), may hold values from -6 to 6
- filter_taps: float32 [8192, 8192], P('ctx', 'tp'), may hold values from -0.0625 to 0.0625
- skip_gain: float32 [8192], P('tp'), may hold values from 0.25 to 2
- out_weight: bfloat16 [8192, 8192], P('tp'), may hold values from -0.0625 to 0.0625
Outputs:
- projected: bfloat16 [8192, 8192], P('ctx', 'tp')
All inputs are finite; a program needn't handle non-finite values.
Results may differ from a plain program's by a relative error of at most 0.0049.
Values sent between devices are 32-bit elements; how exact they have to be, the bound alone decides.
A program may use at most 128 MiB of HBM per device.

v0:
```python
import math

import jax
import jax.numpy as jnp
from jax import lax
from jax.sharding import PartitionSpec as P

PRECISE = lax.Precision.HIGH


def dft_tables(length, sign):
    index = jnp.arange(length, dtype=jnp.int32)
    angle = 2.0 * math.pi / length * (index[:, None] * index[None, :] % length).astype(jnp.float32)
    return (jnp.cos(angle), sign * jnp.sin(angle))


def local_fft(real_part, imag_part, sign):
    length = real_part.shape[-2]
    channels = real_part.shape[-1]
    leading = real_part.shape[:-2]
    bits = length.bit_length() - 1
    first = 2 ** (bits // 2)
    second = length // first
    x_re = real_part.reshape(leading + (first, second, channels))
    x_im = imag_part.reshape(leading + (first, second, channels))
    first_cos, first_sin = dft_tables(first, sign)

    def section_one(matrix, array):
        return jnp.einsum("ca,...abk->...cbk", matrix, array, precision=PRECISE)

    y_re = section_one(first_cos, x_re) - section_one(first_sin, x_im)
    y_im = section_one(first_cos, x_im) + section_one(first_sin, x_re)
    rows_a = jnp.arange(first, dtype=jnp.int32)
    rows_b = jnp.arange(second, dtype=jnp.int32)
    angle = (
        sign
        * 2.0
        * math.pi
        / length
        * (rows_a[:, None] * rows_b[None, :] % length).astype(jnp.float32)
    )
    twist_cos = jnp.cos(angle)[:, :, None]
    twist_sin = jnp.sin(angle)[:, :, None]
    z_re = y_re * twist_cos - y_im * twist_sin
    z_im = y_re * twist_sin + y_im * twist_cos
    second_cos, second_sin = dft_tables(second, sign)

    def section_two(matrix, array):
        return jnp.einsum("db,...cbk->...dck", matrix, array, precision=PRECISE)

    w_re = section_two(second_cos, z_re) - section_two(second_sin, z_im)
    w_im = section_two(second_cos, z_im) + section_two(second_sin, z_re)
    return (w_re.reshape(leading + (length, channels)), w_im.reshape(leading + (length, channels)))


def shards(outer_gate, inner_gate, signal, filter_taps, skip_gain, out_weight):
    gated = inner_gate.astype(jnp.float32) * signal.astype(jnp.float32)
    n_ctx = lax.axis_size("ctx")
    position = lax.axis_index("ctx")
    rows = gated.shape[0]
    span = n_ctx * rows
    block = rows // n_ctx
    stacked = jnp.stack([gated, filter_taps])[:, None]
    spread = lax.all_to_all(stacked, "ctx", split_axis=2, concat_axis=1, tiled=True)
    small_cos, small_sin = dft_tables(n_ctx, -1.0)
    mid_re = jnp.einsum("qp,spjc->sqjc", small_cos, spread, precision=PRECISE)
    mid_im = jnp.einsum("qp,spjc->sqjc", small_sin, spread, precision=PRECISE)
    global_j = position * block + jnp.arange(block, dtype=jnp.int32)
    residues = jnp.arange(n_ctx, dtype=jnp.int32)
    angle = (
        -2.0 * math.pi / span * (residues[:, None] * global_j[None, :] % span).astype(jnp.float32)
    )
    cosine = jnp.cos(angle)[None, :, :, None]
    sine = jnp.sin(angle)[None, :, :, None]
    turned_re = mid_re * cosine - mid_im * sine
    turned_im = mid_re * sine + mid_im * cosine
    owned_re, owned_im = (
        lax.all_to_all(turned_re, "ctx", split_axis=1, concat_axis=2, tiled=True),
        lax.all_to_all(turned_im, "ctx", split_axis=1, concat_axis=2, tiled=True),
    )
    freq_re, freq_im = local_fft(owned_re[:, 0], owned_im[:, 0], -1.0)
    prod_re = freq_re[0] * freq_re[1] - freq_im[0] * freq_im[1]
    prod_im = freq_re[0] * freq_im[1] + freq_im[0] * freq_re[1]
    back_re, back_im = local_fft(prod_re, prod_im, 1.0)
    offsets = jnp.arange(rows, dtype=jnp.int32)
    angle = 2.0 * math.pi / span * (offsets * position % span).astype(jnp.float32)
    cosine = jnp.cos(angle)[:, None]
    sine = jnp.sin(angle)[:, None]
    turned_re = back_re * cosine - back_im * sine
    turned_im = back_re * sine + back_im * cosine
    parts_re, parts_im = (
        lax.all_to_all(turned_re[None], "ctx", split_axis=1, concat_axis=0, tiled=True),
        lax.all_to_all(turned_im[None], "ctx", split_axis=1, concat_axis=0, tiled=True),
    )
    inv_cos, inv_sin = dft_tables(n_ctx, 1.0)
    real_part = jnp.einsum("pq,qjc->pjc", inv_cos, parts_re, precision=PRECISE)
    real_part = real_part - jnp.einsum("pq,qjc->pjc", inv_sin, parts_im, precision=PRECISE)
    placed = lax.all_to_all(real_part, "ctx", split_axis=0, concat_axis=1, tiled=True)
    conv = placed[0] / span
    mixed = (outer_gate.astype(jnp.float32) * (conv + skip_gain * gated)).astype(jnp.bfloat16)
    partial_value = jnp.dot(mixed, out_weight, preferred_element_type=jnp.float32)
    return lax.psum_scatter(partial_value, "tp", scatter_dimension=1, tiled=True).astype(
        jnp.bfloat16
    )


def solution(mesh):
    in_specs = (
        P("ctx", "tp"),
        P("ctx", "tp"),
        P("ctx", "tp"),
        P("ctx", "tp"),
        P("tp"),
        P("tp", None),
    )
    out_specs = P("ctx", "tp")
    return jax.shard_map(shards, mesh=mesh, in_specs=in_specs, out_specs=out_specs, check_vma=False)
```

profile of v0, /device:TPU:1, one launch (start us, length us, event | category | flops | bytes accessed | tf_op | source)
XLA Modules:
  0.0 752.5 jit_solution(2959417799824531095)
XLA Ops:
  6.5 2.1 fusion.42
  9.3 5.2 copy.36
  14.5 9.5 %all-to-all-start = ((f32[2,1,512,1024]{3,0,1,2:T(2,128)}), f32[2,1,512,1024]{3,0,1,2:T(2,128)}, u32[]{:S(2)}, u32[]{:S(2)}) async-start(f32[2,1,512,1024]{3,0,1,2:T(2,128)} %copy.36), calls=%async_computation | async-start | bytes 8388608 | tf_op jit(solution)/shard_map/all_to_all | solution.py:64
  24.2 55.6 %all-to-all-done = f32[2,1,512,1024]{3,0,1,2:T(2,128)} async-done(((f32[2,1,512,1024]{3,0,1,2:T(2,128)}), f32[2,1,512,1024]{3,0,1,2:T(2,128)}, u32[]{:S(2)}, u32[]{:S(2)}) %all-to-all-start) | async-done | bytes 4194336 | tf_op jit(solution)/shard_map/all_to_all | solution.py:64
  79.8 3.5 copy.37
  83.3 4.5 fusion.22
  87.9 8.1 %fusion.2 = (f32[2,16,32,1024]{3,1,2,0:T(8,128)}, f32[2,16,32,1024]{3,1,2,0:T(8,128)S(1)}) fusion(f32[2,32,1024,16]{2,3,1,0:T(8,128)S(1)} %fusion.22, f32[16,32]{0,1:T(8,128)S(1)} %get-tuple-element.16, f32[16,32]{0,1:T(8,128)S(1)} %get-tuple-element.15, f32[2,16,32,1024]{3,2,1,0:T(8,128)S(1)} %bitcast.129), kind=kOutput, calls=%fused_computation.9 | convolution fusion | flops 106958592 | bytes 16781312 | tf_op jit(solution)/shard_map/qp,spjc->sqjc/dot_general | solution.py:67
  96.0 4.4 copy.42
  100.4 6.6 all-to-all-start.2
  107.0 6.6 copy.40
  113.6 49.3 %all-to-all-done.2 = f32[2,16,32,1024]{3,2,0,1:T(8,128)} async-done(((f32[2,16,32,1024]{3,2,0,1:T(8,128)}), f32[2,16,32,1024]{3,2,0,1:T(8,128)}, u32[]{:S(2)}, u32[]{:S(2)}) %all-to-all-start.2) | async-done | bytes 4194336 | tf_op jit(solution)/shard_map/all_to_all | solution.py:79
  162.9 7.0 all-to-all-start.1
  170.2 8.7 %fusion.12 = f32[2,32,1024,16]{2,3,1,0:T(8,128)} fusion(f32[2,16,32,1024]{3,2,0,1:T(8,128)} %all-to-all-done.2), kind=kOutput, calls=%fused_computation.23 | convolution fusion | flops 100666880 | bytes 8388608 | tf_op jit(solution)/shard_map/ca,...abk->...cbk/dot_general | solution.py:29
  178.8 8.7 %fusion.14 = f32[2,32,1024,16]{2,3,1,0:T(8,128)} fusion(f32[2,16,32,1024]{3,2,0,1:T(8,128)} %all-to-all-done.2), kind=kOutput, calls=%fused_computation.25 | convolution fusion | flops 100667136 | bytes 8388608 | tf_op jit(solution)/shard_map/ca,...abk->...cbk/dot_general | solution.py:29
  187.5 37.9 %all-to-all-done.1 = f32[2,16,32,1024]{3,2,0,1:T(8,128)} async-done(((f32[2,16,32,1024]{3,2,0,1:T(8,128)}), f32[2,16,32,1024]{3,2,0,1:T(8,128)}, u32[]{:S(2)}, u32[]{:S(2)}) %all-to-all-start.1) | async-done | bytes 4194336 | tf_op jit(solution)/shard_map/all_to_all | solution.py:78
  225.4 8.4 %fusion.24 = f32[2,32,1024,16]{2,3,1,0:T(8,128)S(1)} fusion(f32[2,32,1024,16]{2,3,1,0:T(8,128)} %fusion.14, f32[2,16,32,1024]{3,2,0,1:T(8,128)} %all-to-all-done.1), kind=kOutput, calls=%fused_computation.35 | convolution fusion | flops 101715456 | bytes 12582912 | tf_op jit(solution)/shard_map/ca,...abk->...cbk/dot_general | solution.py:29
  233.8 8.5 %fusion = (f32[2,16,32,1024]{3,1,2,0:T(8,128)S(1)}, f32[2,16,32,1024]{3,1,2,0:T(8,128)S(1)}) fusion(f32[2,32,1024,16]{2,3,1,0:T(8,128)S(1)} %fusion.24, f32[16,32]{0,1:T(8,128)S(1)} %get-tuple-element.19, f32[16,32]{0,1:T(8,128)S(1)} %get-tuple-element.20, f32[2,32,1024,16]{2,3,1,0:T(8,128)S(1)} %copy-done, f32[2,16,32,1024]{3,2,0,1:T(8,128)} %all-to-all-done.1), kind=kOutput, calls=%fused_computation.3 | convolution fusion | flops 108007168 | bytes 20975616 | tf_op jit(solution)/shard_map/ca,...abk->...cbk/dot_general | solution.py:29
  242.3 5.0 fusion.4
  247.3 4.9 fusion.6
  252.2 5.6 subtract_bitcast_fusion
  257.8 5.1 add_bitcast_fusion
  263.9 1.2 copy.52
  265.1 2.0 fusion.51
  267.1 2.0 fusion.53
  269.1 1.4 copy.50
  270.5 2.0 fusion.59
  272.5 2.5 multiply_subtract_fusion
  275.0 2.2 fusion.43
  277.2 2.2 fusion.45
  279.3 2.2 fusion.65
  281.5 2.4 fusion.68
  284.0 1.2 copy.61
  285.2 1.2 copy.58
  286.4 1.8 fusion.36
  288.3 3.5 copy.64
  291.8 6.6 all-to-all-start.4
  298.4 5.1 copy.62
  303.5 23.5 %all-to-all-done.4 = f32[1,512,1024]{2,0,1:T(1,128)S(1)} async-done(((f32[1,512,1024]{2,0,1:T(1,128)}), f32[1,512,1024]{2,0,1:T(1,128)S(1)}, u32[]{:S(2)}, u32[]{:S(2)}) %all-to-all-start.4) | async-done | bytes 2097184 | tf_op jit(solution)/shard_map/all_to_all | solution.py:93
  327.0 5.5 all-to-all-start.3
  333.2 2.0 fusion.38
  335.2 25.9 %all-to-all-done.3 = f32[1,512,1024]{2,0,1:T(1,128)} async-done(((f32[1,512,1024]{2,0,1:T(1,128)}), f32[1,512,1024]{2,0,1:T(1,128)}, u32[]{:S(2)}, u32[]{:S(2)}) %all-to-all-start.3) | async-done | bytes 2097184 | tf_op jit(solution)/shard_map/all_to_all | solution.py:92
  361.2 2.1 copy.71
  363.2 2.0 fusion.71
  365.3 1.2 copy.66
  366.5 33.5 %all_to_all.63 = f32[16,32,1024]{2,1,0:T(8,128)S(1)} all-to-all(f32[16,32,1024]{2,1,0:T(8,128)S(1)} %copy.66), channel_id=1, replica_groups=mesh['ctx'=16,'tp'=8] {'ctx'}, dimensions={0} | all-to-all | bytes 4194304 | tf_op jit(solution)/shard_map/all_to_all | solution.py:98
  402.7 15.6 %fusion.243 = f32[512,8192]{1,0:T(8,128)} fusion(bf16[512,1024]{1,0:T(8,128)(2,1)S(1)} %fusion.35, bf16[1024,8192]{1,0:T(8,128)(2,1)} %param.11), kind=kOutput, calls=%fused_computation.247 | convolution fusion | flops 8589934592 | bytes 34603008 | tf_op jit(solution)/shard_map/dot_general | solution.py:101
  418.3 324.2 %reduce-scatter.2.cloned.1.call-done = f32[512,1024]{1,0:T(8,128)} async-done(((f32[512,8192]{1,0:T(8,128)}), f32[512,1024]{1,0:T(8,128)}) %reduce-scatter.2.cloned.1.call-update) | async-done | bytes 2097168 | tf_op jit(solution)/shard_map/reduce_scatter | solution.py:102
  742.5 2.7 convert_element_type.122
  (24 shorter events, 5.4 us)
Async XLA Ops:
  6.5 2.2 copy-start.3
  14.5 65.3 %all-to-all-start = ((f32[2,1,512,1024]{3,0,1,2:T(2,128)}), f32[2,1,512,1024]{3,0,1,2:T(2,128)}, u32[]{:S(2)}, u32[]{:S(2)}) async-start(f32[2,1,512,1024]{3,0,1,2:T(2,128)} %copy.36), calls=%async_computation | async-start | bytes 8388608 | tf_op jit(solution)/shard_map/all_to_all | solution.py:64
  100.4 62.5 %all-to-all-start.2 = ((f32[2,16,32,1024]{3,2,0,1:T(8,128)}), f32[2,16,32,1024]{3,2,0,1:T(8,128)}, u32[]{:S(2)}, u32[]{:S(2)}) async-start(f32[2,16,32,1024]{3,2,0,1:T(8,128)} %copy.42), calls=%async_computation.2 | async-start | bytes 8388608 | tf_op jit(solution)/shard_map/all_to_all | solution.py:79
  162.9 62.5 %all-to-all-start.1 = ((f32[2,16,32,1024]{3,2,0,1:T(8,128)}), f32[2,16,32,1024]{3,2,0,1:T(8,128)}, u32[]{:S(2)}, u32[]{:S(2)}) async-start(f32[2,16,32,1024]{3,2,0,1:T(8,128)} %copy.40), calls=%async_computation.1 | async-start | bytes 8388608 | tf_op jit(solution)/shard_map/all_to_all | solution.py:78
  225.4 8.4 %copy-start = (f32[2,32,1024,16]{2,3,1,0:T(8,128)S(1)}, f32[2,32,1024,16]{2,3,1,0:T(8,128)}, u32[]{:S(2)}) copy-start(f32[2,32,1024,16]{2,3,1,0:T(8,128)} %fusion.12) | copy-start | bytes 12582916
  291.8 35.2 %all-to-all-start.4 = ((f32[1,512,1024]{2,0,1:T(1,128)}), f32[1,512,1024]{2,0,1:T(1,128)S(1)}, u32[]{:S(2)}, u32[]{:S(2)}) async-start(f32[1,512,1024]{2,0,1:T(1,128)} %copy.64), calls=%async_computation.4 | async-start | bytes 4194304 | tf_op jit(solution)/shard_map/all_to_all | solution.py:93
  327.0 34.2 %all-to-all-start.3 = ((f32[1,512,1024]{2,0,1:T(1,128)}), f32[1,512,1024]{2,0,1:T(1,128)}, u32[]{:S(2)}, u32[]{:S(2)}) async-start(f32[1,512,1024]{2,0,1:T(1,128)} %copy.62), calls=%async_computation.3 | async-start | bytes 4194304 | tf_op jit(solution)/shard_map/all_to_all | solution.py:92
  332.5 410.0 %reduce-scatter.2.cloned.1.call-start = ((), (), s32[]{:S(2)}) async-start(), calls=%async_computation.7 | async-start | bytes 18874368 | tf_op jit(solution)/shard_map/reduce_scatter | solution.py:102
  400.0 1.2 copy-start.1
  400.0 1.5 copy-start.2
  400.0 1.9 copy-start.4
  400.0 1.9 copy-start.5
Sparse Core Ops, SparseCore 0:
  418.4 323.9 reduce-scatter.1
where the time goes:
time: 757 us; the launch traced here: 752 us
  waiting for transfers between devices  516 us (68%)
  matrix products  104 us (14%)
  local copies, waits for them, and re-layouts  38.9 us (5%)
  starting transfers between devices  35.5 us (5%)
  blocking collectives  33.5 us (4%)
  between operations  14.1 us (2%)
  other arithmetic  9.47 us (1%)
    reduce_scatter x1, waiting for transfers between devices, shards(): lax.psum_scatter(partial_value, 'tp', scatter_dimension=1, tiled=True)  324 us
    all_to_all x1, waiting for transfers between devices, shards(): lax.all_to_all(stacked, 'ctx', split_axis=2, concat_axis=1, tiled=True)  55.6 us
    all_to_all x1, waiting for transfers between devices, shards(): lax.all_to_all(turned_im, 'ctx', split_axis=1, concat_axis=2, tiled=True)  49.3 us
    dot_general x8, matrix products, section_one(): return jnp.einsum('ca,...abk->...cbk', matrix, array, precision=PRECISE)  42.7 us
    all_to_all x1, waiting for transfers between devices, shards(): lax.all_to_all(turned_re, 'ctx', split_axis=1, concat_axis=2, tiled=True)  37.9 us
    all_to_all x1, blocking collectives, shards(): lax.all_to_all(real_part, 'ctx', split_axis=0, concat_axis=1, tiled=True)  33.5 us
    dot_general x8, matrix products, section_two(): return jnp.einsum('db,...cbk->...dck', matrix, array, precision=PRECISE)  29.6 us
    all_to_all x1, waiting for transfers between devices, shards(): lax.all_to_all(turned_re[None], 'ctx', split_axis=1, concat_axis=0, tiled...  25.9 us
  transfers between devices with their start and end apart: 6, of which 6 were waited for; matrix products, arithmetic and copies ran while one was open for 4% of the time, Pallas kernels for 0%

commit v1 on v0

v1 whole, which is shorter than its diff:
```python
import functools
import math

import jax
import jax.numpy as jnp
import numpy as np
from jax import lax
from jax.experimental import pallas as pl
from jax.experimental.pallas import tpu as pltpu
from jax.sharding import PartitionSpec as P

MESH = pl.DeviceIdType.MESH
F32 = jnp.float32
BF16 = jnp.bfloat16

ORDER = ((2, 1), (2, -1), (1, 1), (-1, -1), (1, -1), (-1, 1), (0, 1), (0, -1))
ROWS_A = 224


def split(value):
    high = value.astype(BF16)
    low = (value - high.astype(F32)).astype(BF16)
    return high, low


def split_np(value):
    value = np.asarray(value, np.float64)
    high = value.astype(BF16)
    low = (value - high.astype(np.float64)).astype(BF16)
    return np.stack([high, low])


def tables():
    n1 = np.arange(64)[None, :]
    k1 = np.arange(32)[:, None]
    cos = np.cos(2 * np.pi * (n1 * k1 % 64) / 64)
    sin = np.sin(2 * np.pi * (n1 * k1 % 64) / 64)
    ahead = np.stack([cos, -sin], axis=1)
    ahead[0, 1] = (-1.0) ** np.arange(64)
    ahead = ahead.reshape(64, 64)
    back = np.stack([2 * cos, -2 * sin], axis=1)
    back[0, 0] = 1.0
    back[0, 1] = (-1.0) ** np.arange(64)
    back = back.reshape(64, 64).T / 8192
    eye = np.eye(8)
    n2 = np.arange(128)
    angle = 2 * np.pi * (n2[:, None] * n2[None, :] % 128) / 128
    c, s = np.cos(angle), np.sin(angle)
    fwd = np.block([[c, s], [-s, c]])
    inv = np.block([[c, -s], [s, c]])
    turn = 2 * np.pi * (n2[:, None] * np.arange(33)[None, :]) / 8192
    twist = np.zeros((128, 128))
    twist[:, :33] = np.cos(turn)
    twist[:, 64:97] = np.sin(turn)
    return (
        split_np(np.kron(ahead, eye)),
        split_np(np.kron(back, eye)),
        split_np(fwd),
        split_np(inv),
        twist.astype(np.float32),
    )


def dot3(matrix_ref, value):
    high, low = split(value)
    big, small = matrix_ref[0], matrix_ref[1]
    total = jnp.dot(big, low, preferred_element_type=F32)
    total += jnp.dot(small, high, preferred_element_type=F32)
    return total + jnp.dot(big, high, preferred_element_type=F32)


def here():
    ctx, tp = lax.axis_index("ctx"), lax.axis_index("tp")
    return ctx, tp


def conv_kernel(
    inner_ref, signal_ref, taps_ref, skip_ref, outer_hbm, ahead_hbm, back_hbm, fwd_hbm, inv_hbm, twist_hbm,
    mixed_ref,
    send, recv, spec, prod, result, home,
    outer_ref, ahead_ref, back_ref, fwd_ref, inv_ref, twist_ref,
    load_sem, out_send, out_recv, back_send, back_recv,
):
    ctx, tp = here()
    z_hi, x, core, z_lo = ctx // 8, (ctx // 2) % 4, ctx % 2, tp % 2
    z = 2 * z_hi + z_lo
    partner_tp = tp + 1 - 2 * z_lo
    sign = 1 - 2 * core

    loads = []
    for i, (src, dst) in enumerate(
        (
            (ahead_hbm, ahead_ref), (fwd_hbm, fwd_ref), (inv_hbm, inv_ref),
            (back_hbm, back_ref), (twist_hbm, twist_ref), (outer_hbm, outer_ref),
        )
    ):
        copy = pltpu.make_async_copy(src, dst, load_sem.at[i])
        copy.start()
        loads.append(copy)

    quads = []
    for dx, dz in ORDER:
        to_z = (z + dz * sign + 4) % 4
        quads.append((to_z // 2) * 4 + (x + dx * sign + 4) % 4)

    barrier = pltpu.get_barrier_semaphore()
    for q in quads:
        for k in (0, 1):
            pl.semaphore_signal(barrier, inc=1, device_id=(2 * q + k, partner_tp), device_id_type=MESH)

    lane = lax.broadcasted_iota(jnp.int32, (128, 128), 1)
    first = lane < 64
    row0 = lax.broadcasted_iota(jnp.int32, (128, 128), 0)
    sends = []
    for step, q in enumerate(quads):
        columns = pl.ds(pl.multiple_of(q * 128, 128), 128)
        skip = skip_ref[:, columns]

        def pack(i, carry, columns=columns, skip=skip, q=q):
            rows = pl.ds(pl.multiple_of(i * 128, 128), 128)
            gated = inner_ref[rows, columns].astype(F32) * signal_ref[rows, columns].astype(F32)
            tap0 = jnp.logical_and(row0 + i * 128 + ctx * 512 == 0, True)
            taps = taps_ref[rows, columns] + jnp.where(tap0, skip, 0.0)
            send[2 * q, rows, :] = jnp.where(first, gated, pltpu.roll(taps, 64, 1))
            send[2 * q + 1, rows, :] = jnp.where(first, pltpu.roll(gated, 64, 1), taps)
            return carry

        lax.fori_loop(0, 4, pack, 0)
        if step == 0:
            pl.semaphore_wait(barrier, 16)
        for dk in (0, 1):
            k = (core + dk) % 2
            copy = pltpu.make_async_remote_copy(
                send.at[2 * q + k], recv.at[ctx],
                out_send.at[2 * step + dk], out_recv.at[2 * step + dk],
                device_id=(2 * q + k, partner_tp), device_id_type=MESH,
            )
            copy.start()
            sends.append(copy)
    for copy in loads:
        copy.wait()
    for copy in sends:
        copy.wait_recv()

    first8 = lax.broadcasted_iota(jnp.int32, (8, 128), 1) < 64

    def stage_one(a, carry):
        near = recv.at[:, :, :]
        parts = []
        for half in (0, 1):
            start = pl.multiple_of(half * 64 + a * 8, 8)
            parts.append(
                jnp.concatenate(
                    [
                        recv[s, pl.ds(pl.multiple_of(j * 128 + start, 8), 8), :]
                        for s in range(16)
                        for j in range(4)
                    ],
                    axis=0,
                )
            )
        out = dot3(ahead_ref, jnp.concatenate(parts, axis=1))
        for half in (0, 1):
            rows = pl.ds(pl.multiple_of(half * 64 + a * 8, 8), 8)
            twist = twist_ref[rows, :]
            for k1 in range(33):
                if k1 == 0:
                    spec[0, 0, rows, :] = out[0:8, half * 128 : half * 128 + 128]
                    spec[0, 1, rows, :] = jnp.zeros((8, 128), F32)
                    continue
                cos, sin = twist[:, k1 : k1 + 1], twist[:, 64 + k1 : 65 + k1]
                if k1 == 32:
                    real = out[8:16, half * 128 : half * 128 + 128]
                    spec[32, 0, rows, :] = real * cos
                    spec[32, 1, rows, :] = -(real * sin)
                    continue
                real = out[16 * k1 : 16 * k1 + 8, half * 128 : half * 128 + 128]
                imag = out[16 * k1 + 8 : 16 * k1 + 16, half * 128 : half * 128 + 128]
                spec[k1, 0, rows, :] = real * cos + imag * sin
                spec[k1, 1, rows, :] = imag * cos - real * sin
        return carry

    lax.fori_loop(0, 8, stage_one, 0)

    def product(out, j):
        real, imag = out[:128, 128 * j : 128 * j + 128], out[128:, 128 * j : 128 * j + 128]
        real2, imag2 = pltpu.roll(real, 64, 1), pltpu.roll(imag, 64, 1)
        return jnp.concatenate([real * real2 - imag * imag2, real * imag2 + imag * real2], axis=0)

    first256 = lax.broadcasted_iota(jnp.int32, (256, 128), 1) < 64

    def stage_two(i, carry):
        value = jnp.concatenate([spec[4 * i + j].reshape(256, 128) for j in range(4)], axis=1)
        out = dot3(fwd_ref, value)
        pairs = [
            jnp.where(first256, product(out, 2 * j), product(out, 2 * j + 1)) for j in range(2)
        ]
        out = dot3(inv_ref, jnp.concatenate(pairs, axis=1))
        for j in range(2):
            prod[2 * i + j] = out[:, 128 * j : 128 * j + 128].reshape(2, 128, 128)
        return carry

    lax.fori_loop(0, 8, stage_two, 0)
    out = dot3(fwd_ref, spec[32].reshape(256, 128))
    prod[16] = dot3(inv_ref, product(out, 0)).reshape(2, 128, 128)

    def stage_three(a2, carry):
        sides = []
        for side in (0, 1):
            a = 2 * a2 + side
            low = pl.ds(pl.multiple_of(a * 8, 8), 8)
            high = pl.ds(pl.multiple_of(64 + a * 8, 8), 8)
            near, far = twist_ref[low, :], twist_ref[high, :]

            def turn(k1):
                cos = jnp.where(first8, near[:, k1 : k1 + 1], far[:, k1 : k1 + 1])
                sin = jnp.where(first8, near[:, 64 + k1 : 65 + k1], far[:, 64 + k1 : 65 + k1])
                return cos, sin

            pieces = []
            for pair in range(16):
                here_re, here_im = prod[pair, 0, low, :], prod[pair, 1, low, :]
                next_re, next_im = prod[pair, 0, high, :], prod[pair, 1, high, :]
                for odd in (0, 1):
                    k1 = 2 * pair + odd
                    if odd:
                        real = jnp.where(first8, pltpu.roll(here_re, 64, 1), next_re)
                        imag = jnp.where(first8, pltpu.roll(here_im, 64, 1), next_im)
                    else:
                        real = jnp.where(first8, here_re, pltpu.roll(next_re, 64, 1))
                        imag = jnp.where(first8, here_im, pltpu.roll(next_im, 64, 1))
                    if k1 == 0:
                        pieces.append(real)
                        real = jnp.where(first8, prod[16, 0, low, :], prod[16, 0, high, :])
                        imag = jnp.where(first8, prod[16, 1, low, :], prod[16, 1, high, :])
                        cos, sin = turn(32)
                        pieces.append(real * cos - imag * sin)
                        continue
                    cos, sin = turn(k1)
                    pieces.append(real * cos - imag * sin)
                    pieces.append(real * sin + imag * cos)
            sides.append(jnp.concatenate(pieces, axis=0))
        out = dot3(back_ref, jnp.concatenate(sides, axis=1))
        for side in (0, 1):
            rows = pl.ds(pl.multiple_of((2 * a2 + side) * 8, 8), 8)
            result[:, rows, :] = out[:, 128 * side : 128 * side + 128].reshape(64, 8, 128)
        return carry

    lax.fori_loop(0, 4, stage_three, 0)

    returns = []
    for step, q in enumerate(quads):
        for dk in (0, 1):
            other = 2 * q + (core + dk) % 2
            copy = pltpu.make_async_remote_copy(
                result.at[pl.ds(4 * other, 4)], home.at[ctx],
                back_send.at[2 * step + dk], back_recv.at[2 * step + dk],
                device_id=(other, partner_tp), device_id_type=MESH,
            )
            copy.start()
            returns.append(copy)
    for copy in returns:
        copy.wait_recv()
    first64 = lax.broadcasted_iota(jnp.int32, (64, 128), 1) < 64
    for q in range(8):

        def gate(j, carry, q=q):
            even, odd = home[2 * q, j], home[2 * q + 1, j]
            base = pl.multiple_of(j * 128, 128)
            for rows, conv in (
                (pl.ds(base, 64), jnp.where(first64, even, pltpu.roll(odd, 64, 1))),
                (pl.ds(base + 64, 64), jnp.where(first64, pltpu.roll(even, 64, 1), odd)),
            ):
                gated = outer_ref[rows, 128 * q : 128 * q + 128].astype(F32) * conv
                mixed_ref[rows, 128 * q : 128 * q + 128] = gated.astype(BF16)
            return carry

        lax.fori_loop(0, 4, gate, 0)
    for copy in sends + returns:
        copy.wait_send()


def convolve(outer, inner, signal, taps, skip):
    ahead, back, fwd, inv, twist = tables()
    vmem = pl.BlockSpec(memory_space=pltpu.VMEM)
    hbm = pl.BlockSpec(memory_space=pl.ANY)
    dma = pltpu.SemaphoreType.DMA
    return pl.pallas_call(
        conv_kernel,
        name="convolve",
        out_shape=jax.ShapeDtypeStruct((512, 1024), BF16),
        in_specs=[vmem] * 4 + [hbm] * 6,
        out_specs=vmem,
        scratch_shapes=[
            pltpu.VMEM((16, 512, 128), F32),
            pltpu.VMEM((16, 512, 128), F32),
            pltpu.VMEM((33, 2, 128, 128), F32),
            pltpu.VMEM((17, 2, 128, 128), F32),
            pltpu.VMEM((64, 64, 128), F32),
            pltpu.VMEM((16, 4, 64, 128), F32),
            pltpu.VMEM((512, 1024), BF16),
            pltpu.VMEM((2, 512, 512), BF16),
            pltpu.VMEM((2, 512, 512), BF16),
            pltpu.VMEM((2, 256, 256), BF16),
            pltpu.VMEM((2, 256, 256), BF16),
            pltpu.VMEM((128, 128), F32),
            dma((6,)), dma((16,)), dma((16,)), dma((16,)), dma((16,)),
        ],
        compiler_params=pltpu.CompilerParams(
            collective_id=0, has_side_effects=True, vmem_limit_bytes=56 << 20
        ),
    )(inner, signal, taps, skip.reshape(1, -1), outer, ahead, back, fwd, inv, twist)


def project_kernel(
    mixed_ref, weight_hbm, out_ref,
    weight, part, in_b, in_a, in_za, in_zb,
    load_sem, yb_send, yb_recv, ya_send, ya_recv, za_send, za_recv, zb_send, zb_recv,
):
    ctx, tp = here()
    y, z_lo = tp // 2, tp % 2
    na = ROWS_A
    rows_a, rows_b = pl.ds(0, na), pl.ds(na, 512 - na)
    up = (ctx, 2 * ((y + 1) % 4) + z_lo)
    down = (ctx, 2 * ((y + 3) % 4) + z_lo)
    across = (ctx, tp + 1 - 2 * z_lo)
    blocks = [(2, 0), (1, 0), (3, 0), (0, 0), (2, 1), (1, 1), (3, 1), (0, 1)]

    loads = []
    for i, (r, w) in enumerate(blocks):
        other = z_lo if w else 1 - z_lo
        start = pl.multiple_of((2 * ((y + r) % 4) + other) * 1024, 1024)
        copy = pltpu.make_async_copy(weight_hbm.at[:, pl.ds(start, 1024)], weight.at[i], load_sem.at[i])
        copy.start()
        loads.append(copy)
    barrier = pltpu.get_barrier_semaphore()
    for device in (up, down, across):
        pl.semaphore_signal(barrier, inc=1, device_id=device, device_id_type=MESH)

    def remote(src, dst, send_sem, recv_sem, device):
        copy = pltpu.make_async_remote_copy(
            src, dst, send_sem, recv_sem, device_id=device, device_id_type=MESH
        )
        copy.start()
        return copy

    started = []
    arrive = {}

    def ring(tag, rows, w, m, direction):
        r = 2 if m == 0 else (1 if direction == 0 else 3)
        half = (direction if m in (0, 2) else 1 - direction)
        src = part.at[r, w, pl.ds(2 * half, 2), rows, :]
        slot = 2 * m + direction
        device = up if direction == 0 else down
        if tag == "a":
            copy = remote(src, in_a.at[slot], ya_send.at[slot], ya_recv.at[slot], device)
        else:
            copy = remote(src, in_b.at[w, slot], yb_send.at[w, slot], yb_recv.at[w, slot], device)
        started.append(copy)
        arrive[tag, w, m, direction] = copy

    def across_a(r):
        copy = remote(part.at[r, 0, :, rows_a, :], in_za.at[r], za_send.at[r], za_recv.at[r], across)
        started.append(copy)
        arrive["z", r] = copy

    for i, (r, w) in enumerate(blocks):
        loads[i].wait()

        def tile(j, carry, i=i, r=r, w=w):
            columns = pl.ds(pl.multiple_of(j * 256, 256), 256)
            part[r, w, j] = jnp.dot(mixed_ref[...], weight[i, :, columns], preferred_element_type=F32)
            return carry

        lax.fori_loop(0, 4, tile, 0)
        if i == 0:
            pl.semaphore_wait(barrier, 3)
        if r == 2:
            ring("b", rows_b, w, 0, 0)
            ring("b", rows_b, w, 0, 1)
        elif r == 1:
            ring("b", rows_b, w, 1, 0)
        elif r == 3:
            ring("b", rows_b, w, 1, 1)
        if w == 0:
            across_a(r)

    def add(target, rows, source):
        target[:, rows, :] = target[:, rows, :] + source[...]

    def pass_on(tag, rows, w, inbox):
        for direction, r in ((0, 1), (1, 3)):
            arrive[tag, w, 0, direction].wait_recv()
            add(part.at[r, w, pl.ds(2 * direction, 2)], rows, inbox.at[direction])
            ring(tag, rows, w, 2, direction)

    pass_on("b", rows_b, 0, in_b.at[0])
    pass_on("b", rows_b, 1, in_b.at[1])

    def join_a(r):
        arrive["z", r].wait_recv()
        add(part.at[r, 1], rows_a, in_za.at[r])

    join_a(2)
    ring("a", rows_a, 1, 0, 0)
    ring("a", rows_a, 1, 0, 1)
    join_a(1)
    ring("a", rows_a, 1, 1, 0)
    join_a(3)
    ring("a", rows_a, 1, 1, 1)

    def gather(tag, w, rows, inbox):
        for m in (1, 2):
            for direction in (0, 1):
                arrive[tag, w, m, direction].wait_recv()
                half = direction if m == 2 else 1 - direction
                add(part.at[0, w, pl.ds(2 * half, 2)], rows, inbox.at[2 * m + direction])

    gather("b", 0, rows_b, in_b.at[0])
    last = remote(part.at[0, 0, :, rows_b, :], in_zb, zb_send, zb_recv, across)
    started.append(last)
    join_a(0)
    pass_on("a", rows_a, 1, in_a)
    gather("b", 1, rows_b, in_b.at[1])
    last.wait_recv()
    for j in range(4):
        out_ref[rows_b, 256 * j : 256 * j + 256] = (part[0, 1, j, rows_b, :] + in_zb[j]).astype(BF16)
    gather("a", 1, rows_a, in_a)
    for j in range(4):
        out_ref[rows_a, 256 * j : 256 * j + 256] = part[0, 1, j, rows_a, :].astype(BF16)
    for copy in started:
        copy.wait_send()


def project(mixed, weight):
    vmem = pl.BlockSpec(memory_space=pltpu.VMEM)
    dma = pltpu.SemaphoreType.DMA
    na, nb = ROWS_A, 512 - ROWS_A
    return pl.pallas_call(
        project_kernel,
        name="project",
        out_shape=jax.ShapeDtypeStruct((512, 1024), BF16),
        in_specs=[vmem, pl.BlockSpec(memory_space=pl.ANY)],
        out_specs=vmem,
        scratch_shapes=[
            pltpu.VMEM((8, 1024, 1024), BF16),
            pltpu.VMEM((4, 2, 4, 512, 256), F32),
            pltpu.VMEM((2, 6, 2, nb, 256), F32),
            pltpu.VMEM((6, 2, na, 256), F32),
            pltpu.VMEM((4, 4, na, 256), F32),
            pltpu.VMEM((4, nb, 256), F32),
            dma((8,)), dma((2, 6)), dma((2, 6)), dma((6,)), dma((6,)),
            dma((4,)), dma((4,)), dma, dma,
        ],
        compiler_params=pltpu.CompilerParams(
            collective_id=1, has_side_effects=True, vmem_limit_bytes=60 << 20
        ),
    )(mixed, weight)


def shards(outer_gate, inner_gate, signal, filter_taps, skip_gain, out_weight):
    mixed = convolve(outer_gate, inner_gate, signal, filter_taps, skip_gain)
    return project(mixed, out_weight)


def solution(mesh):
    in_specs = (
        P("ctx", "tp"),
        P("ctx", "tp"),
        P("ctx", "tp"),
        P("ctx", "tp"),
        P("tp"),
        P("tp", None),
    )
    return jax.shard_map(shards, mesh=mesh, in_specs=in_specs, out_specs=P("ctx", "tp"), check_vma=False)
```

time: 757 us -> 224 us (0.30)
  waiting for transfers between devices: 516 us -> 0 us
  Pallas kernels: 0 us -> 222 us
  matrix products: 104 us -> 0 us
  local copies, waits for them, and re-layouts: 38.9 us -> 2.26 us
  starting transfers between devices: 35.5 us -> 0 us
  blocking collectives: 33.5 us -> 0 us
  between operations: 14.1 us -> 0.02 us
  other arithmetic: 9.47 us -> 0 us
    reduce_scatter x1 -> x0, waiting for transfers between devices: 324 us -> none  [shards(): lax.psum_scatter(partial_value, 'tp', scatter_dimension=1, tiled=True)]
    pallas_call x0 -> x2, Pallas kernels: none -> 222 us  [the longest x1 115 us: project(): pl.pallas_call(project_kernel, name='project', out_shape=jax.ShapeDtypeSt...]
    all_to_all x5 -> x0, waiting for transfers between devices: 192 us -> none  [the longest x1 55.6 us: shards(): lax.all_to_all(stacked, 'ctx', split_axis=2, concat_axis=1, tiled=True)]
    dot_general x21 -> x0, matrix products: 104 us -> none  [the longest x8 42.7 us: section_one(): return jnp.einsum('ca,...abk->...cbk', matrix, array, precision=PRECISE)]
    all_to_all x5 -> x0, starting transfers between devices: 35.2 us -> none  [the longest x1 9.49 us: shards(): lax.all_to_all(stacked, 'ctx', split_axis=2, concat_axis=1, tiled=True)]
    all_to_all x1 -> x0, blocking collectives: 33.5 us -> none  [shards(): lax.all_to_all(real_part, 'ctx', split_axis=0, concat_axis=1, tiled=True)]
    sub x5 -> x0, local copies, waits for them, and re-layouts: 15.5 us -> none  [the longest x1 6.6 us: shards(): turned_re = mid_re * cosine - mid_im * sine]
    add x4 -> x0, local copies, waits for them, and re-layouts: 10.3 us -> none  [the longest x1 4.37 us: shards(): turned_im = mid_re * sine + mid_im * cosine]
  transfers between devices with their start and end apart: 6 -> 0, of which waited for: 6 -> 0; matrix products, arithmetic and copies ran while one was open for 4% -> 0% of each run, Pallas kernels for 0% -> 0%
where the time goes in v1:
time: 224 us
  Pallas kernels  222 us (99%)
  local copies, waits for them, and re-layouts  2.26 us (1%)
    pallas_call x1, Pallas kernels, project(): pl.pallas_call(project_kernel, name='project', out_shape=jax.ShapeDtypeSt...  115 us
    pallas_call x1, Pallas kernels, convolve(): pl.pallas_call(conv_kernel, name='convolve', out_shape=jax.ShapeDtypeStru...  106 us

profile of v1, /device:TPU:1, one launch (start us, length us, event | category | flops | bytes accessed | tf_op | source)
XLA Modules:
  0.0 223.8 jit_solution(8468771520728931839)
XLA Ops:
  0.0 106.3 %convolve.1.mixed_ref = bf16[512,1024]{1,0:T(8,128)(2,1)} custom-call(bf16[512,1024]{1,0:T(8,128)(2,1)} %inner_ref.1, bf16[512,1024]{1,0:T(8,128)(2,1)} %signal_ref.1, f32[512,1024]{1,0:T(8,128)} %taps_ref.1, f32[1,1024]{1,0:T(1,128)} %bitcast.1, bf16[512,1024]{1,0:T(8,128)(2,1)} %outer_hbm.1, bf16[2,512,512]{2,1,0:T(8,128)(2,1)} %constant.10.clone.ahead_hbm, ...), custom_call_target="tpu_custom_call" | custom-call | tf_op jit(solution)/shard_map/convolve/pallas_call | solution.py:288
  106.3 115.2 %project.1 = bf16[512,1024]{1,0:T(8,128)(2,1)} custom-call(bf16[512,1024]{1,0:T(8,128)(2,1)} %convolve.1.mixed_ref, bf16[1024,8192]{1,0:T(8,128)(2,1)} %weight_hbm.1), custom_call_target="tpu_custom_call" | custom-call | tf_op jit(solution)/shard_map/project/pallas_call | solution.py:440
  221.5 2.3 %copy.13 = bf16[512,1024]{1,0:T(8,128)(2,1)} copy(bf16[512,1024]{1,0:T(8,128)(2,1)} %project.1) | data formatting | bytes 2097152

commit v2 on v1

v2 whole, which is shorter than its diff:
```python
import functools
import math

import jax
import jax.numpy as jnp
import numpy as np
from jax import lax
from jax.experimental import pallas as pl
from jax.experimental.pallas import tpu as pltpu
from jax.sharding import PartitionSpec as P

MESH = pl.DeviceIdType.MESH
F32 = jnp.float32
BF16 = jnp.bfloat16

ORDER = ((2, 1), (2, -1), (1, 1), (-1, -1), (1, -1), (-1, 1), (0, 1), (0, -1))
SETS = {"b1": (0, 128), "b2": (128, 192), "a": (320, 192)}


def split(value):
    high = value.astype(BF16)
    low = (value - high.astype(F32)).astype(BF16)
    return high, low


def split_np(value):
    value = np.asarray(value, np.float64)
    high = value.astype(BF16)
    low = (value - high.astype(np.float64)).astype(BF16)
    return np.stack([high, low])


def tables():
    n1 = np.arange(64)[None, :]
    k1 = np.arange(32)[:, None]
    cos = np.cos(2 * np.pi * (n1 * k1 % 64) / 64)
    sin = np.sin(2 * np.pi * (n1 * k1 % 64) / 64)
    ahead = np.stack([cos, -sin], axis=1)
    ahead[0, 1] = (-1.0) ** np.arange(64)
    ahead = ahead.reshape(64, 64)
    back = np.stack([2 * cos, -2 * sin], axis=1)
    back[0, 0] = 1.0
    back[0, 1] = (-1.0) ** np.arange(64)
    back = back.reshape(64, 64).T / 8192
    back = back.reshape(16, 4, 64).transpose(1, 0, 2).reshape(64, 64)
    eye = np.eye(8)
    n2 = np.arange(128)
    angle = 2 * np.pi * (n2[:, None] * n2[None, :] % 128) / 128
    c, s = np.cos(angle), np.sin(angle)
    fwd = np.block([[c, s], [-s, c]])
    inv = np.block([[c, -s], [s, c]])
    turn = 2 * np.pi * (n2[:, None] * np.arange(33)[None, :]) / 8192
    twist = np.zeros((128, 128))
    twist[:, :33] = np.cos(turn)
    twist[:, 64:97] = np.sin(turn)
    return (
        split_np(np.kron(ahead, eye)),
        split_np(np.kron(back, eye)),
        split_np(fwd),
        split_np(inv),
        twist.astype(np.float32),
    )


def dot3(matrix_ref, value):
    high, low = split(value)
    big, small = matrix_ref[0], matrix_ref[1]
    total = jnp.dot(big, low, preferred_element_type=F32)
    total += jnp.dot(small, high, preferred_element_type=F32)
    return total + jnp.dot(big, high, preferred_element_type=F32)


def here():
    ctx, tp = lax.axis_index("ctx"), lax.axis_index("tp")
    return ctx, tp


SEND, RECV, SPEC, PROD, TAPS = 0, 16, 32, 49, 32
BLOCKS = ((2, 0), (1, 0), (3, 0), (0, 0), (2, 1), (1, 1), (3, 1), (0, 1))


def layer_kernel(
    skip_ref, inner_hbm, signal_hbm, taps_hbm, outer_hbm, weight_hbm,
    ahead_hbm, back_hbm, fwd_hbm, inv_hbm, twist_hbm,
    out_ref,
    work, weight, result, home, mixed_ref,
    outer_ref, ahead_ref, back_ref, fwd_ref, inv_ref, twist_ref,
    in_b1, in_b2, in_a, in_za, in_zb1, in_zb2,
    in_sem, load_sem, weight_sem, out_send, out_recv, back_send, back_recv,
    y_send, y_recv, z_send, z_recv,
):
    ctx, tp = here()
    z_hi, x, core = ctx // 8, (ctx // 2) % 4, ctx % 2
    y, z_lo = tp // 2, tp % 2
    z = 2 * z_hi + z_lo
    partner_tp = tp + 1 - 2 * z_lo
    sign = 1 - 2 * core
    up = (ctx, 2 * ((y + 1) % 4) + z_lo)
    down = (ctx, 2 * ((y + 3) % 4) + z_lo)
    across = (ctx, partner_tp)

    quads = []
    for dx, dz in ORDER:
        to_z = (z + dz * sign + 4) % 4
        quads.append((to_z // 2) * 4 + (x + dx * sign + 4) % 4)

    arrays = []
    for step, q in enumerate(quads):
        columns = pl.ds(pl.multiple_of(q * 128, 128), 128)
        copies = [
            pltpu.make_async_copy(
                inner_hbm.at[:, columns], weight.at[7, pl.ds(0, 512), pl.ds(128 * step, 128)], in_sem.at[step, 0]
            ),
            pltpu.make_async_copy(
                signal_hbm.at[:, columns], weight.at[7, pl.ds(512, 512), pl.ds(128 * step, 128)], in_sem.at[step, 1]
            ),
            pltpu.make_async_copy(taps_hbm.at[:, columns], work.at[TAPS + step], in_sem.at[step, 2]),
        ]
        for copy in copies:
            copy.start()
        arrays.append(copies)

    barrier = pltpu.get_barrier_semaphore()
    for q in quads:
        for k in (0, 1):
            pl.semaphore_signal(barrier, inc=1, device_id=(2 * q + k, partner_tp), device_id_type=MESH)
    for device in (up, down):
        pl.semaphore_signal(barrier, inc=1, device_id=device, device_id_type=MESH)

    loads = []
    for i, (src, dst) in enumerate(
        (
            (ahead_hbm, ahead_ref), (fwd_hbm, fwd_ref), (inv_hbm, inv_ref),
            (back_hbm, back_ref), (twist_hbm, twist_ref), (outer_hbm, outer_ref),
        )
    ):
        copy = pltpu.make_async_copy(src, dst, load_sem.at[i])
        copy.start()
        loads.append(copy)

    def load_weight(i):
        r, w = BLOCKS[i]
        other = z_lo if w else 1 - z_lo
        start = pl.multiple_of((2 * ((y + r) % 4) + other) * 1024, 1024)
        copy = pltpu.make_async_copy(weight_hbm.at[:, pl.ds(start, 1024)], weight.at[i], weight_sem.at[i])
        copy.start()
        return copy

    weights = [load_weight(i) for i in range(7)]

    lane = lax.broadcasted_iota(jnp.int32, (128, 128), 1)
    first = lane < 64
    row0 = lax.broadcasted_iota(jnp.int32, (128, 128), 0)
    sends = []
    for step, q in enumerate(quads):
        skip = skip_ref[:, pl.ds(pl.multiple_of(q * 128, 128), 128)]
        for copy in arrays[step]:
            copy.wait()

        def pack(i, carry, step=step, skip=skip, q=q):
            start = pl.multiple_of(i * 128, 128)
            rows = pl.ds(start, 128)
            columns = pl.ds(128 * step, 128)
            gated = weight[7, rows, columns].astype(F32) * weight[7, pl.ds(512 + start, 128), columns].astype(F32)
            taps = work[TAPS + step, rows, :] + jnp.where(row0 + i * 128 + ctx * 512 == 0, skip, 0.0)
            work[SEND + 2 * q, rows, :] = jnp.where(first, gated, pltpu.roll(taps, 64, 1))
            work[SEND + 2 * q + 1, rows, :] = jnp.where(first, pltpu.roll(gated, 64, 1), taps)
            return carry

        lax.fori_loop(0, 4, pack, 0)
        if step == 0:
            pl.semaphore_wait(barrier, 18)
        for dk in (0, 1):
            k = (core + dk) % 2
            copy = pltpu.make_async_remote_copy(
                work.at[SEND + 2 * q + k], work.at[RECV + ctx],
                out_send.at[2 * step + dk], out_recv.at[2 * step + dk],
                device_id=(2 * q + k, partner_tp), device_id_type=MESH,
            )
            copy.start()
            sends.append(copy)
    weights.append(load_weight(7))
    for copy in loads:
        copy.wait()
    for copy in sends:
        copy.wait_recv()

    first8 = lax.broadcasted_iota(jnp.int32, (8, 128), 1) < 64

    def put_spec(k1, part, half, a, value):
        start = (k1 % 2) * 256 + part * 128 + half * 64 + a * 8
        work[SPEC + k1 // 2, pl.ds(pl.multiple_of(start, 8), 8), :] = value

    def prod_at(pair, part, rows):
        start = (pair % 2) * 256 + part * 128 + rows
        return work[PROD + pair // 2, pl.ds(pl.multiple_of(start, 8), 8), :]

    def stage_one(a, carry):
        parts = []
        for half in (0, 1):
            start = pl.multiple_of(half * 64 + a * 8, 8)
            parts.append(
                jnp.concatenate(
                    [
                        work[RECV + s, pl.ds(pl.multiple_of(j * 128 + start, 8), 8), :]
                        for s in range(16)
                        for j in range(4)
                    ],
                    axis=0,
                )
            )
        out = dot3(ahead_ref, jnp.concatenate(parts, axis=1))
        for half in (0, 1):
            rows = pl.ds(pl.multiple_of(half * 64 + a * 8, 8), 8)
            twist = twist_ref[rows, :]
            for k1 in range(33):
                if k1 == 0:
                    put_spec(0, 0, half, a, out[0:8, half * 128 : half * 128 + 128])
                    put_spec(0, 1, half, a, jnp.zeros((8, 128), F32))
                    continue
                cos, sin = twist[:, k1 : k1 + 1], twist[:, 64 + k1 : 65 + k1]
                if k1 == 32:
                    real = out[8:16, half * 128 : half * 128 + 128]
                    put_spec(32, 0, half, a, real * cos)
                    put_spec(32, 1, half, a, -(real * sin))
                    continue
                real = out[16 * k1 : 16 * k1 + 8, half * 128 : half * 128 + 128]
                imag = out[16 * k1 + 8 : 16 * k1 + 16, half * 128 : half * 128 + 128]
                put_spec(k1, 0, half, a, real * cos + imag * sin)
                put_spec(k1, 1, half, a, imag * cos - real * sin)
        return carry

    lax.fori_loop(0, 8, stage_one, 0)

    def product(out, j):
        real, imag = out[:128, 128 * j : 128 * j + 128], out[128:, 128 * j : 128 * j + 128]
        real2, imag2 = pltpu.roll(real, 64, 1), pltpu.roll(imag, 64, 1)
        return jnp.concatenate([real * real2 - imag * imag2, real * imag2 + imag * real2], axis=0)

    first256 = lax.broadcasted_iota(jnp.int32, (256, 128), 1) < 64

    def stage_two(i, carry):
        value = jnp.concatenate([work[SPEC + 2 * i + j // 2, 256 * (j % 2) : 256 * (j % 2) + 256, :] for j in range(4)], axis=1)
        out = dot3(fwd_ref, value)
        pairs = [
            jnp.where(first256, product(out, 2 * j), product(out, 2 * j + 1)) for j in range(2)
        ]
        out = dot3(inv_ref, jnp.concatenate(pairs, axis=1))
        for j in range(2):
            work[PROD + i, 256 * j : 256 * j + 256, :] = out[:, 128 * j : 128 * j + 128]
        return carry

    lax.fori_loop(0, 8, stage_two, 0)
    out = dot3(fwd_ref, work[SPEC + 16, 0:256, :])
    work[PROD + 8, 0:256, :] = dot3(inv_ref, product(out, 0))

    def stage_three(a2, carry):
        sides = []
        for side in (0, 1):
            a = 2 * a2 + side
            low = pl.ds(pl.multiple_of(a * 8, 8), 8)
            high = pl.ds(pl.multiple_of(64 + a * 8, 8), 8)
            near, far = twist_ref[low, :], twist_ref[high, :]

            def turn(k1):
                cos = jnp.where(first8, near[:, k1 : k1 + 1], far[:, k1 : k1 + 1])
                sin = jnp.where(first8, near[:, 64 + k1 : 65 + k1], far[:, 64 + k1 : 65 + k1])
                return cos, sin

            pieces = []
            for pair in range(16):
                here_re, here_im = prod_at(pair, 0, a * 8), prod_at(pair, 1, a * 8)
                next_re, next_im = prod_at(pair, 0, 64 + a * 8), prod_at(pair, 1, 64 + a * 8)
                for odd in (0, 1):
                    k1 = 2 * pair + odd
                    if odd:
                        real = jnp.where(first8, pltpu.roll(here_re, 64, 1), next_re)
                        imag = jnp.where(first8, pltpu.roll(here_im, 64, 1), next_im)
                    else:
                        real = jnp.where(first8, here_re, pltpu.roll(next_re, 64, 1))
                        imag = jnp.where(first8, here_im, pltpu.roll(next_im, 64, 1))
                    if k1 == 0:
                        pieces.append(real)
                        real = jnp.where(first8, prod_at(16, 0, a * 8), prod_at(16, 0, 64 + a * 8))
                        imag = jnp.where(first8, prod_at(16, 1, a * 8), prod_at(16, 1, 64 + a * 8))
                        cos, sin = turn(32)
                        pieces.append(real * cos - imag * sin)
                        continue
                    cos, sin = turn(k1)
                    pieces.append(real * cos - imag * sin)
                    pieces.append(real * sin + imag * cos)
            sides.append(jnp.concatenate(pieces, axis=0))
        out = dot3(back_ref, jnp.concatenate(sides, axis=1))
        for side in (0, 1):
            rows = pl.ds(pl.multiple_of((2 * a2 + side) * 8, 8), 8)
            result[:, :, rows, :] = out[:, 128 * side : 128 * side + 128].reshape(4, 16, 8, 128)
        return carry

    lax.fori_loop(0, 4, stage_three, 0)

    for copy in sends:
        copy.wait_send()
    returns = [[], []]
    for part, (begin, count) in enumerate(((0, 1), (1, 3))):
        for step, q in enumerate(quads):
            for dk in (0, 1):
                other = 2 * q + (core + dk) % 2
                copy = pltpu.make_async_remote_copy(
                    result.at[pl.ds(begin, count), other], home.at[ctx, pl.ds(begin, count)],
                    back_send.at[part, 2 * step + dk], back_recv.at[part, 2 * step + dk],
                    device_id=(other, partner_tp), device_id_type=MESH,
                )
                copy.start()
                returns[part].append(copy)

    first64 = lax.broadcasted_iota(jnp.int32, (64, 128), 1) < 64

    def gate(j, carry):
        base = pl.multiple_of(j * 128, 128)
        for q in range(8):
            even, odd = home[2 * q, j], home[2 * q + 1, j]
            for rows, conv in (
                (pl.ds(base, 64), jnp.where(first64, even, pltpu.roll(odd, 64, 1))),
                (pl.ds(base + 64, 64), jnp.where(first64, pltpu.roll(even, 64, 1), odd)),
            ):
                gated = outer_ref[rows, 128 * q : 128 * q + 128].astype(F32) * conv
                mixed_ref[rows, 128 * q : 128 * q + 128] = gated.astype(BF16)
        return carry

    started = []
    arrive = {}
    inboxes = {"b1": in_b1, "b2": in_b2, "a": in_a}
    lane_of = {("b1", 0): 0, ("b1", 1): 1, ("b2", 0): 2, ("b2", 1): 3, ("a", 1): 4}

    def rows_of(name):
        return pl.ds(*SETS[name])

    def slots(r, w, half=None):
        block = 8 * BLOCKS.index((r, w))
        return pl.ds(block, 8) if half is None else pl.ds(block + 4 * half, 4)

    def inbox(name, w, slot):
        return in_a.at[slot] if name == "a" else inboxes[name].at[w, slot]

    def remote(src, dst, send_sem, recv_sem, device):
        copy = pltpu.make_async_remote_copy(
            src, dst, send_sem, recv_sem, device_id=device, device_id_type=MESH
        )
        copy.start()
        started.append(copy)
        return copy

    def ring(name, w, m, direction):
        r = 2 if m == 0 else (1 if direction == 0 else 3)
        half = direction if m in (0, 2) else 1 - direction
        slot = 2 * m + direction
        at = lane_of[name, w]
        arrive[name, w, m, direction] = remote(
            work.at[slots(r, w, half), rows_of(name), :], inbox(name, w, slot),
            y_send.at[at, slot], y_recv.at[at, slot], up if direction == 0 else down,
        )

    def own(name, i):
        r, w = BLOCKS[i]
        if r == 2:
            ring(name, w, 0, 0)
            ring(name, w, 0, 1)
        elif r == 1:
            ring(name, w, 1, 0)
        elif r == 3:
            ring(name, w, 1, 1)

    def across_a(r):
        arrive["z", r] = remote(
            work.at[slots(r, 0), rows_of("a"), :], in_za.at[r], z_send.at[r], z_recv.at[r], across
        )

    def multiply(i, begin, count):
        def tile(j, carry):
            columns = pl.ds(pl.multiple_of(j * 256, 256), 256)
            rows = pl.ds(begin, count)
            value = jnp.dot(mixed_ref[rows, :], weight[i, :, columns], preferred_element_type=F32)
            work[8 * i + 2 * j, rows, :] = value[:, :128]
            work[8 * i + 2 * j + 1, rows, :] = value[:, 128:]
            return carry

        lax.fori_loop(0, 4, tile, 0)

    def add(target, name, source):
        rows = rows_of(name)
        work[target, rows, :] = work[target, rows, :] + source[...]

    def pass_on(name, w):
        for direction, r in ((0, 1), (1, 3)):
            arrive[name, w, 0, direction].wait_recv()
            add(slots(r, w, direction), name, inbox(name, w, direction))
            ring(name, w, 2, direction)

    def join_a(r):
        arrive["z", r].wait_recv()
        add(slots(r, 1), "a", in_za.at[r])

    def gather(name, w):
        for m in (1, 2):
            for direction in (0, 1):
                arrive[name, w, m, direction].wait_recv()
                half = direction if m == 2 else 1 - direction
                add(slots(0, w, half), name, inbox(name, w, 2 * m + direction))

    def across_b(name, box, at):
        return remote(work.at[slots(0, 0), rows_of(name), :], box, z_send.at[at], z_recv.at[at], across)

    def finish(name, box=None):
        rows = rows_of(name)
        for j in range(8):
            value = work[8 * BLOCKS.index((0, 1)) + j, rows, :]
            if box is not None:
                value = value + box[j]
            out_ref[rows, 128 * j : 128 * j + 128] = value.astype(BF16)

    for copy in returns[0]:
        copy.wait_recv()
    lax.fori_loop(0, 1, gate, 0)
    for i in range(8):
        weights[i].wait()
        multiply(i, 0, 128)
        own("b1", i)
    for copy in returns[1]:
        copy.wait_recv()
    lax.fori_loop(1, 4, gate, 0)
    for i in range(8):
        multiply(i, 128, 384)
        if BLOCKS[i][1] == 0:
            across_a(BLOCKS[i][0])
        own("b2", i)
        if i == 1:
            pass_on("b1", 0)
    pass_on("b1", 1)
    pass_on("b2", 0)
    join_a(2)
    ring("a", 1, 0, 0)
    ring("a", 1, 0, 1)
    gather("b1", 0)
    last1 = across_b("b1", in_zb1, 4)
    pass_on("b2", 1)
    join_a(1)
    ring("a", 1, 1, 0)
    join_a(3)
    ring("a", 1, 1, 1)
    gather("b1", 1)
    gather("b2", 0)
    last2 = across_b("b2", in_zb2, 5)
    last1.wait_recv()
    finish("b1", in_zb1)
    join_a(0)
    pass_on("a", 1)
    gather("b2", 1)
    last2.wait_recv()
    finish("b2", in_zb2)
    gather("a", 1)
    finish("a")
    for copy in returns[0] + returns[1] + started:
        copy.wait_send()


def shards(outer_gate, inner_gate, signal, filter_taps, skip_gain, out_weight):
    vmem = pl.BlockSpec(memory_space=pltpu.VMEM)
    hbm = pl.BlockSpec(memory_space=pl.ANY)
    dma = pltpu.SemaphoreType.DMA
    n1, n2, na = SETS["b1"][1], SETS["b2"][1], SETS["a"][1]
    return pl.pallas_call(
        layer_kernel,
        name="layer",
        out_shape=jax.ShapeDtypeStruct((512, 1024), BF16),
        in_specs=[vmem] + [hbm] * 10,
        out_specs=vmem,
        scratch_shapes=[
            pltpu.VMEM((64, 512, 128), F32),
            pltpu.VMEM((8, 1024, 1024), BF16),
            pltpu.VMEM((4, 16, 64, 128), F32),
            pltpu.VMEM((16, 4, 64, 128), F32),
            pltpu.VMEM((512, 1024), BF16),
            pltpu.VMEM((512, 1024), BF16),
            pltpu.VMEM((2, 512, 512), BF16),
            pltpu.VMEM((2, 512, 512), BF16),
            pltpu.VMEM((2, 256, 256), BF16),
            pltpu.VMEM((2, 256, 256), BF16),
            pltpu.VMEM((128, 128), F32),
            pltpu.VMEM((2, 6, 4, n1, 128), F32),
            pltpu.VMEM((2, 6, 4, n2, 128), F32),
            pltpu.VMEM((6, 4, na, 128), F32),
            pltpu.VMEM((4, 8, na, 128), F32),
            pltpu.VMEM((8, n1, 128), F32),
            pltpu.VMEM((8, n2, 128), F32),
            dma((8, 3)), dma((6,)), dma((8,)), dma((16,)), dma((16,)), dma((2, 16)), dma((2, 16)),
            dma((5, 6)), dma((5, 6)), dma((6,)), dma((6,)),
        ],
        compiler_params=pltpu.CompilerParams(
            collective_id=0, has_side_effects=True, vmem_limit_bytes=62 << 20
        ),
    )(
        skip_gain.reshape(1, -1), inner_gate, signal, filter_taps, outer_gate, out_weight, *tables(),
    )


def solution(mesh):
    in_specs = (
        P("ctx", "tp"),
        P("ctx", "tp"),
        P("ctx", "tp"),
        P("ctx", "tp"),
        P("tp"),
        P("tp", None),
    )
    return jax.shard_map(shards, mesh=mesh, in_specs=in_specs, out_specs=P("ctx", "tp"), check_vma=False)
```

time: 224 us -> 206 us (0.920)
  Pallas kernels: 222 us -> 203 us
    pallas_call x2 -> x1, Pallas kernels: 222 us -> 203 us  [shards(): pl.pallas_call(layer_kernel, name='layer', out_shape=jax.ShapeDtypeStruct...]
where the time goes in v2:
time: 206 us
  Pallas kernels  203 us (99%)
  local copies, waits for them, and re-layouts  2.26 us (1%)
    pallas_call x1, Pallas kernels, shards(): pl.pallas_call(layer_kernel, name='layer', out_shape=jax.ShapeDtypeStruct...  203 us

profile of v2, /device:TPU:1, one launch (start us, length us, event | category | flops | bytes accessed | tf_op | source)
XLA Modules:
  0.0 205.6 jit_solution(8168638994980099070)
XLA Ops:
  0.0 203.3 %layer.1 = bf16[512,1024]{1,0:T(8,128)(2,1)} custom-call(f32[1,1024]{1,0:T(1,128)} %bitcast.1, bf16[512,1024]{1,0:T(8,128)(2,1)} %inner_hbm.1, bf16[512,1024]{1,0:T(8,128)(2,1)} %signal_hbm.1, f32[512,1024]{1,0:T(8,128)} %taps_hbm.1, bf16[512,1024]{1,0:T(8,128)(2,1)} %outer_hbm.1, bf16[1024,8192]{1,0:T(8,128)(2,1)} %weight_hbm.1, ...), custom_call_target="tpu_custom_call" | custom-call | tf_op jit(solution)/shard_map/layer/pallas_call | solution.py:471
  203.3 2.3 %copy.13 = bf16[512,1024]{1,0:T(8,128)(2,1)} copy(bf16[512,1024]{1,0:T(8,128)(2,1)} %layer.1) | data formatting | bytes 2097152

commit v3 on v2

--- a/solution.py
+++ b/solution.py
@@ -14,7 +14,11 @@
 BF16 = jnp.bfloat16
 
 ORDER = ((2, 1), (2, -1), (1, 1), (-1, -1), (1, -1), (-1, 1), (0, 1), (0, -1))
-SETS = {"b1": (0, 128), "b2": (128, 192), "a": (320, 192)}
+SETS = {"b": (0, 128), "a1": (128, 128), "a2": (256, 128), "a3": (384, 128)}
+AS = ("a1", "a2", "a3")
+UNITS = ((2, 0), (2, 1), (1, 1), (3, 0), (1, 0), (3, 1), (0, 0), (0, 1))
+SLOT = {2: 0, 1: 1, 3: 2, 0: 3}
+BY_Z = (True, True, False, False, False, False, True, True)
 
 
 def split(value):
@@ -82,12 +86,12 @@
 def layer_kernel(
     skip_ref, inner_hbm, signal_hbm, taps_hbm, outer_hbm, weight_hbm,
     ahead_hbm, back_hbm, fwd_hbm, inv_hbm, twist_hbm,
-    out_ref,
-    work, weight, result, home, mixed_ref,
+    out_hbm, wide,
+    work, weight, result, home, mixed_ref, out_ref,
     outer_ref, ahead_ref, back_ref, fwd_ref, inv_ref, twist_ref,
-    in_b1, in_b2, in_a, in_za, in_zb1, in_zb2,
-    in_sem, load_sem, weight_sem, out_send, out_recv, back_send, back_recv,
-    y_send, y_recv, z_send, z_recv,
+    in_b, in_a, in_zb, give, take, other_mixed, share,
+    in_sem, load_sem, weight_sem, wide_sem, out_sem, out_send, out_recv, back_send, back_recv,
+    y_send, y_recv, z_send, z_recv, wz_send, wz_recv, wx_send, wx_recv, wc_send, wc_recv,
 ):
     ctx, tp = here()
     z_hi, x, core = ctx // 8, (ctx // 2) % 4, ctx % 2
@@ -98,6 +102,9 @@
     up = (ctx, 2 * ((y + 1) % 4) + z_lo)
     down = (ctx, 2 * ((y + 3) % 4) + z_lo)
     across = (ctx, partner_tp)
+    sides = [(8 * ((z + d) % 4 // 2) + 2 * x + core, partner_tp) for d in (1, 3)]
+    rights = [(8 * z_hi + 2 * ((x + d) % 4) + core, tp) for d in (1, 3, 2)]
+    twin = (ctx + sign, tp)
 
     quads = []
     for dx, dz in ORDER:
@@ -124,7 +131,7 @@
     for q in quads:
         for k in (0, 1):
             pl.semaphore_signal(barrier, inc=1, device_id=(2 * q + k, partner_tp), device_id_type=MESH)
-    for device in (up, down):
+    for device in [up, down, twin] + rights:
         pl.semaphore_signal(barrier, inc=1, device_id=device, device_id_type=MESH)
 
     loads = []
@@ -169,7 +176,7 @@
 
         lax.fori_loop(0, 4, pack, 0)
         if step == 0:
-            pl.semaphore_wait(barrier, 18)
+            pl.semaphore_wait(barrier, 22)
         for dk in (0, 1):
             k = (core + dk) % 2
             copy = pltpu.make_async_remote_copy(
@@ -182,8 +189,82 @@
     weights.append(load_weight(7))
     for copy in loads:
         copy.wait()
+    mine = [pl.multiple_of(256 * ((x + d) % 4) + 128 * core + 64 * z_hi, 64) for d in (0, 2)]
+    for i in range(4):
+        weights[i].wait()
+    for u, (r, half) in enumerate(UNITS):
+        for c in range(4):
+            columns = slice(512 * half + 128 * c, 512 * half + 128 * c + 128)
+            for p in (0, 1):
+                share[u, p, c] = weight[SLOT[r], pl.ds(mine[p], 64), columns].astype(F32)
     for copy in sends:
         copy.wait_recv()
+
+    started = []
+
+    def remote(src, dst, send_sem, recv_sem, device):
+        copy = pltpu.make_async_remote_copy(
+            src, dst, send_sem, recv_sem, device_id=device, device_id_type=MESH
+        )
+        copy.start()
+        started.append(copy)
+        return copy
+
+    wz, wx, wc = {}, {}, {}
+
+    def give_z(u):
+        for p in range(1 + BY_Z[u]):
+            for h in (0, 1):
+                wz[u, p, h] = remote(
+                    share.at[u, p], wide.at[u, :, pl.ds(mine[p], 64)],
+                    wz_send.at[u, 2 * p + h], wz_recv.at[u, 2 * p + h], sides[h],
+                )
+
+    def quarter(u, d):
+        return wide.at[u, :, pl.ds(pl.multiple_of(256 * ((x + d) % 4) + 128 * core, 128), 128)]
+
+    def give_core(u, d):
+        wc[u, d] = remote(quarter(u, d), quarter(u, d), wc_send.at[u, d], wc_recv.at[u, d], twin)
+
+    def spread(u):
+        for h in (0, 1):
+            wz[u, 0, h].wait_recv()
+        for n in range(3 - BY_Z[u]):
+            wx[u, n] = remote(quarter(u, 0), quarter(u, 0), wx_send.at[u, n], wx_recv.at[u, n], rights[n])
+        give_core(u, 0)
+        if BY_Z[u]:
+            for h in (0, 1):
+                wz[u, 1, h].wait_recv()
+            give_core(u, 2)
+
+    def pair_up(u):
+        for n, d in enumerate((3, 1) if BY_Z[u] else (3, 1, 2)):
+            wx[u, n].wait_recv()
+            give_core(u, d)
+
+    def fetch(u):
+        for n in range(4):
+            wc[u, n].wait_recv()
+        copy = pltpu.make_async_copy(wide.at[u], (result, home)[u % 2], wide_sem.at[u])
+        copy.start()
+        return copy
+
+    def settle(u, copy):
+        copy.wait()
+        r, half = UNITS[u]
+        box = (result, home)[u % 2]
+
+        def convert(i, carry):
+            rows = pl.ds(pl.multiple_of(i * 128, 128), 128)
+            for c in range(4):
+                columns = slice(512 * half + 128 * c, 512 * half + 128 * c + 128)
+                weight[SLOT[r], rows, columns] = box[c, rows, :].astype(BF16)
+            return carry
+
+        lax.fori_loop(0, 8, convert, 0)
+
+    for u in range(5):
+        give_z(u)
 
     first8 = lax.broadcasted_iota(jnp.int32, (8, 128), 1) < 64
 
@@ -250,7 +331,10 @@
             work[PROD + i, 256 * j : 256 * j + 256, :] = out[:, 128 * j : 128 * j + 128]
         return carry
 
-    lax.fori_loop(0, 8, stage_two, 0)
+    lax.fori_loop(0, 4, stage_two, 0)
+    spread(0)
+    lax.fori_loop(4, 8, stage_two, 0)
+    spread(1)
     out = dot3(fwd_ref, work[SPEC + 16, 0:256, :])
     work[PROD + 8, 0:256, :] = dot3(inv_ref, product(out, 0))
 
@@ -292,45 +376,58 @@
             sides.append(jnp.concatenate(pieces, axis=0))
         out = dot3(back_ref, jnp.concatenate(sides, axis=1))
         for side in (0, 1):
-            rows = pl.ds(pl.multiple_of((2 * a2 + side) * 8, 8), 8)
-            result[:, :, rows, :] = out[:, 128 * side : 128 * side + 128].reshape(4, 16, 8, 128)
+            value = out[:, 128 * side : 128 * side + 128].reshape(4, 16, 8, 128)
+            for s in range(16):
+                result[:, pl.ds(pl.multiple_of(64 * s + (2 * a2 + side) * 8, 8), 8), :] = value[:, s]
         return carry
 
     lax.fori_loop(0, 4, stage_three, 0)
 
     for copy in sends:
         copy.wait_send()
-    returns = [[], []]
-    for part, (begin, count) in enumerate(((0, 1), (1, 3))):
+    returns = [[], [], [], []]
+
+    def give_back(part):
         for step, q in enumerate(quads):
             for dk in (0, 1):
                 other = 2 * q + (core + dk) % 2
                 copy = pltpu.make_async_remote_copy(
-                    result.at[pl.ds(begin, count), other], home.at[ctx, pl.ds(begin, count)],
+                    result.at[part, pl.ds(pl.multiple_of(64 * other, 64), 64)],
+                    home.at[part, pl.ds(pl.multiple_of(64 * ctx, 64), 64)],
                     back_send.at[part, 2 * step + dk], back_recv.at[part, 2 * step + dk],
                     device_id=(other, partner_tp), device_id_type=MESH,
                 )
                 copy.start()
                 returns[part].append(copy)
 
+    def receive(part):
+        for copy in returns[part]:
+            copy.wait_recv()
+
+    give_back(0)
+    give_back(1)
+    receive(0)
+    give_back(2)
     first64 = lax.broadcasted_iota(jnp.int32, (64, 128), 1) < 64
 
-    def gate(j, carry):
+    def gate(j, carry, keep=True):
         base = pl.multiple_of(j * 128, 128)
         for q in range(8):
-            even, odd = home[2 * q, j], home[2 * q + 1, j]
+            even, odd = home[j, 128 * q : 128 * q + 64, :], home[j, 128 * q + 64 : 128 * q + 128, :]
             for rows, conv in (
                 (pl.ds(base, 64), jnp.where(first64, even, pltpu.roll(odd, 64, 1))),
                 (pl.ds(base + 64, 64), jnp.where(first64, pltpu.roll(even, 64, 1), odd)),
             ):
                 gated = outer_ref[rows, 128 * q : 128 * q + 128].astype(F32) * conv
-                mixed_ref[rows, 128 * q : 128 * q + 128] = gated.astype(BF16)
+                rounded = gated.astype(BF16)
+                mixed_ref[rows, 128 * q : 128 * q + 128] = rounded
+                if keep:
+                    begin = 64 * (rows.start != base)
+                    give[j - 1, pl.ds(begin, 64), 128 * q : 128 * q + 128] = rounded.astype(F32)
         return carry
 
-    started = []
     arrive = {}
-    inboxes = {"b1": in_b1, "b2": in_b2, "a": in_a}
-    lane_of = {("b1", 0): 0, ("b1", 1): 1, ("b2", 0): 2, ("b2", 1): 3, ("a", 1): 4}
+    lane_of = {("b", 0): 0, ("b", 1): 1, ("a1", 1): 2, ("a2", 1): 3, ("a3", 1): 4}
 
     def rows_of(name):
         return pl.ds(*SETS[name])
@@ -340,15 +437,7 @@
         return pl.ds(block, 8) if half is None else pl.ds(block + 4 * half, 4)
 
     def inbox(name, w, slot):
-        return in_a.at[slot] if name == "a" else inboxes[name].at[w, slot]
-
-    def remote(src, dst, send_sem, recv_sem, device):
-        copy = pltpu.make_async_remote_copy(
-            src, dst, send_sem, recv_sem, device_id=device, device_id_type=MESH
-        )
-        copy.start()
-        started.append(copy)
-        return copy
+        return in_b.at[w, slot] if name == "b" else in_a.at[AS.index(name), slot]
 
     def ring(name, w, m, direction):
         r = 2 if m == 0 else (1 if direction == 0 else 3)
@@ -370,11 +459,6 @@
         elif r == 3:
             ring(name, w, 1, 1)
 
-    def across_a(r):
-        arrive["z", r] = remote(
-            work.at[slots(r, 0), rows_of("a"), :], in_za.at[r], z_send.at[r], z_recv.at[r], across
-        )
-
     def multiply(i, begin, count):
         def tile(j, carry):
             columns = pl.ds(pl.multiple_of(j * 256, 256), 256)
@@ -386,19 +470,34 @@
 
         lax.fori_loop(0, 4, tile, 0)
 
+    def complete(u, names):
+        r, half = UNITS[u]
+        begin, count = SETS[names[0]][0], 128 * len(names)
+        block = 8 * BLOCKS.index((r, 1)) + 4 * half
+        for j in range(2):
+            columns = slice(512 * half + 256 * j, 512 * half + 256 * j + 256)
+            value = jnp.dot(
+                other_mixed[begin - 128 : begin - 128 + count, :], weight[SLOT[r], :, columns],
+                preferred_element_type=F32,
+            )
+            rows = pl.ds(begin, count)
+            work[block + 2 * j, rows, :] = work[block + 2 * j, rows, :] + value[:, :128]
+            work[block + 2 * j + 1, rows, :] = work[block + 2 * j + 1, rows, :] + value[:, 128:]
+
+    def accept(name):
+        arrive["z", name].wait_recv()
+        at = AS.index(name)
+        other_mixed[128 * at : 128 * at + 128, :] = take[at].astype(BF16)
+
     def add(target, name, source):
         rows = rows_of(name)
         work[target, rows, :] = work[target, rows, :] + source[...]
 
-    def pass_on(name, w):
-        for direction, r in ((0, 1), (1, 3)):
+    def pass_on(name, w, directions=(0, 1)):
+        for direction in directions:
             arrive[name, w, 0, direction].wait_recv()
-            add(slots(r, w, direction), name, inbox(name, w, direction))
+            add(slots((1, 3)[direction], w, direction), name, inbox(name, w, direction))
             ring(name, w, 2, direction)
-
-    def join_a(r):
-        arrive["z", r].wait_recv()
-        add(slots(r, 1), "a", in_za.at[r])
 
     def gather(name, w):
         for m in (1, 2):
@@ -407,8 +506,7 @@
                 half = direction if m == 2 else 1 - direction
                 add(slots(0, w, half), name, inbox(name, w, 2 * m + direction))
 
-    def across_b(name, box, at):
-        return remote(work.at[slots(0, 0), rows_of(name), :], box, z_send.at[at], z_recv.at[at], across)
+    writes = []
 
     def finish(name, box=None):
         rows = rows_of(name)
@@ -417,68 +515,125 @@
             if box is not None:
                 value = value + box[j]
             out_ref[rows, 128 * j : 128 * j + 128] = value.astype(BF16)
-
-    for copy in returns[0]:
-        copy.wait_recv()
-    lax.fori_loop(0, 1, gate, 0)
+        copy = pltpu.make_async_copy(out_ref.at[rows], out_hbm.at[rows], out_sem.at[len(writes)])
+        copy.start()
+        writes.append(copy)
+
+    gate(0, 0, keep=False)
+
+    def offer(at):
+        gate(at + 1, 0)
+        arrive["z", AS[at]] = remote(give.at[at], take.at[at], z_send.at[at], z_recv.at[at], across)
+
     for i in range(8):
-        weights[i].wait()
+        if i > 3:
+            weights[i].wait()
         multiply(i, 0, 128)
-        own("b1", i)
-    for copy in returns[1]:
-        copy.wait_recv()
-    lax.fori_loop(1, 4, gate, 0)
-    for i in range(8):
+        own("b", i)
+        if i == 3:
+            receive(1)
+            give_back(3)
+            offer(0)
+    pair_up(0)
+    pair_up(1)
+    pass_on("b", 0)
+    receive(2)
+    offer(1)
+    spread(2)
+    receive(3)
+    spread(3)
+    offer(2)
+    spread(4)
+    give_z(5)
+    give_z(6)
+    give_z(7)
+    for part in returns:
+        for copy in part:
+            copy.wait_send()
+    first0, first1 = fetch(0), fetch(1)
+    for i in range(4, 8):
         multiply(i, 128, 384)
-        if BLOCKS[i][1] == 0:
-            across_a(BLOCKS[i][0])
-        own("b2", i)
-        if i == 1:
-            pass_on("b1", 0)
-    pass_on("b1", 1)
-    pass_on("b2", 0)
-    join_a(2)
-    ring("a", 1, 0, 0)
-    ring("a", 1, 0, 1)
-    gather("b1", 0)
-    last1 = across_b("b1", in_zb1, 4)
-    pass_on("b2", 1)
-    join_a(1)
-    ring("a", 1, 1, 0)
-    join_a(3)
-    ring("a", 1, 1, 1)
-    gather("b1", 1)
-    gather("b2", 0)
-    last2 = across_b("b2", in_zb2, 5)
-    last1.wait_recv()
-    finish("b1", in_zb1)
-    join_a(0)
-    pass_on("a", 1)
-    gather("b2", 1)
-    last2.wait_recv()
-    finish("b2", in_zb2)
-    gather("a", 1)
-    finish("a")
-    for copy in returns[0] + returns[1] + started:
+    pass_on("b", 1)
+    settle(0, first0)
+    settle(1, first1)
+
+    def first_step(name):
+        accept(name)
+        complete(0, [name])
+        ring(name, 1, 0, 0)
+        complete(1, [name])
+        ring(name, 1, 0, 1)
+
+    first_step("a1")
+    pair_up(2)
+    settle(2, fetch(2))
+    complete(2, ["a1"])
+    ring("a1", 1, 1, 0)
+    gather("b", 0)
+    last = remote(work.at[slots(0, 0), rows_of("b"), :], in_zb, z_send.at[3], z_recv.at[3], across)
+    first_step("a2")
+    complete(2, ["a2"])
+    ring("a2", 1, 1, 0)
+    pair_up(3)
+    settle(3, fetch(3))
+    complete(3, ["a1", "a2"])
+    ring("a1", 1, 1, 1)
+    ring("a2", 1, 1, 1)
+    first_step("a3")
+    complete(2, ["a3"])
+    ring("a3", 1, 1, 0)
+    complete(3, ["a3"])
+    ring("a3", 1, 1, 1)
+    spread(5)
+    pair_up(4)
+    settle(4, fetch(4))
+    complete(4, AS)
+    for name in AS:
+        pass_on(name, 1, (0,))
+    spread(6)
+    pair_up(5)
+    settle(5, fetch(5))
+    complete(5, AS)
+    for name in AS:
+        pass_on(name, 1, (1,))
+    spread(7)
+    pair_up(6)
+    pair_up(7)
+    gather("b", 1)
+    last.wait_recv()
+    finish("b", in_zb)
+    settle(6, fetch(6))
+    complete(6, AS)
+    settle(7, fetch(7))
+    complete(7, AS)
+    for name in AS:
+        gather(name, 1)
+        finish(name)
+    for copy in started:
         copy.wait_send()
+    for copy in writes:
+        copy.wait()
 
 
 def shards(outer_gate, inner_gate, signal, filter_taps, skip_gain, out_weight):
     vmem = pl.BlockSpec(memory_space=pltpu.VMEM)
     hbm = pl.BlockSpec(memory_space=pl.ANY)
     dma = pltpu.SemaphoreType.DMA
-    n1, n2, na = SETS["b1"][1], SETS["b2"][1], SETS["a"][1]
-    return pl.pallas_call(
+    projected, _ = pl.pallas_call(
         layer_kernel,
         name="layer",
-        out_shape=jax.ShapeDtypeStruct((512, 1024), BF16),
+        out_shape=(
+            jax.ShapeDtypeStruct((512, 1024), BF16),
+            jax.ShapeDtypeStruct((8, 4, 1024, 128), F32),
+        ),
         in_specs=[vmem] + [hbm] * 10,
-        out_specs=vmem,
+        out_specs=(hbm, hbm),
         scratch_shapes=[
             pltpu.VMEM((64, 512, 128), F32),
             pltpu.VMEM((8, 1024, 1024), BF16),
-            pltpu.VMEM((4, 16, 64, 128), F32),
-            pltpu.VMEM((16, 4, 64, 128), F32),
+            pltpu.VMEM((4, 1024, 128), F32),
+            pltpu.VMEM((4, 1024, 128), F32),
+            pltpu.VMEM((512, 1024), BF16),
             pltpu.VMEM((512, 1024), BF16),
             pltpu.VMEM((512, 1024), BF16),
             pltpu.VMEM((2, 512, 512), BF16),
@@ -486,14 +641,17 @@
             pltpu.VMEM((2, 256, 256), BF16),
             pltpu.VMEM((2, 256, 256), BF16),
             pltpu.VMEM((128, 128), F32),
-            pltpu.VMEM((2, 6, 4, n1, 128), F32),
-            pltpu.VMEM((2, 6, 4, n2, 128), F32),
-            pltpu.VMEM((6, 4, na, 128), F32),
-            pltpu.VMEM((4, 8, na, 128), F32),
-            pltpu.VMEM((8, n1, 128), F32),
-            pltpu.VMEM((8, n2, 128), F32),
-            dma((8, 3)), dma((6,)), dma((8,)), dma((16,)), dma((16,)), dma((2, 16)), dma((2, 16)),
-            dma((5, 6)), dma((5, 6)), dma((6,)), dma((6,)),
+            pltpu.VMEM((2, 6, 4, 128, 128), F32),
+            pltpu.VMEM((3, 6, 4, 128, 128), F32),
+            pltpu.VMEM((8, 128, 128), F32),
+            pltpu.VMEM((3, 128, 1024), F32),
+            pltpu.VMEM((3, 128, 1024), F32),
+            pltpu.VMEM((384, 1024), BF16),
+            pltpu.VMEM((8, 2, 4, 64, 128), F32),
+            dma((8, 3)), dma((6,)), dma((8,)), dma((8,)), dma((4,)),
+            dma((16,)), dma((16,)), dma((4, 16)), dma((4, 16)),
+            dma((5, 6)), dma((5, 6)), dma((4,)), dma((4,)),
+            dma((8, 4)), dma((8, 4)), dma((8, 3)), dma((8, 3)), dma((8, 4)), dma((8, 4)),
         ],
         compiler_params=pltpu.CompilerParams(
             collective_id=0, has_side_effects=True, vmem_limit_bytes=62 << 20
@@ -501,6 +659,7 @@
     )(
         skip_gain.reshape(1, -1), inner_gate, signal, filter_taps, outer_gate, out_weight, *tables(),
     )
+    return projected
 
 
 def solution(mesh):

time: 206 us -> 183 us (0.89)
  Pallas kernels: 203 us -> 181 us
    pallas_call x1, Pallas kernels: 203 us -> 181 us  [shards(): pl.pallas_call(layer_kernel, name='layer', out_shape=(jax.ShapeDtypeStruc...]
where the time goes in v3:
time: 183 us
  Pallas kernels  181 us (99%)
  local copies, waits for them, and re-layouts  2.26 us (1%)
    pallas_call x1, Pallas kernels, shards(): pl.pallas_call(layer_kernel, name='layer', out_shape=(jax.ShapeDtypeStruc...  181 us

profile of v3, /device:TPU:1, one launch (start us, length us, event | category | flops | bytes accessed | tf_op | source)
XLA Modules:
  0.0 182.9 jit_solution(849771171856753315)
XLA Ops:
  0.0 180.6 %layer.1 = (bf16[512,1024]{1,0:T(8,128)(2,1)}, f32[8,4,1024,128]{3,2,1,0:T(8,128)}) custom-call(f32[1,1024]{1,0:T(1,128)} %bitcast.1, bf16[512,1024]{1,0:T(8,128)(2,1)} %inner_hbm.1, bf16[512,1024]{1,0:T(8,128)(2,1)} %signal_hbm.1, f32[512,1024]{1,0:T(8,128)} %taps_hbm.1, bf16[512,1024]{1,0:T(8,128)(2,1)} %outer_hbm.1, bf16[1024,8192]{1,0:T(8,128)(2,1)} %weight_hbm.1, ...), custom_call_target="tpu_custom_call" | custom-call | tf_op jit(solution)/shard_map/layer/pallas_call | solution.py:622
  180.6 2.3 %copy.13 = bf16[512,1024]{1,0:T(8,128)(2,1)} copy(bf16[512,1024]{1,0:T(8,128)(2,1)} %get-tuple-element.6) | data formatting | bytes 2097152

commit v4 on v3

--- a/solution.py
+++ b/solution.py
@@ -18,7 +18,6 @@
 AS = ("a1", "a2", "a3")
 UNITS = ((2, 0), (2, 1), (1, 1), (3, 0), (1, 0), (3, 1), (0, 0), (0, 1))
 SLOT = {2: 0, 1: 1, 3: 2, 0: 3}
-BY_Z = (True, True, False, False, False, False, True, True)
 
 
 def split(value):
@@ -103,7 +102,7 @@
     down = (ctx, 2 * ((y + 3) % 4) + z_lo)
     across = (ctx, partner_tp)
     sides = [(8 * ((z + d) % 4 // 2) + 2 * x + core, partner_tp) for d in (1, 3)]
-    rights = [(8 * z_hi + 2 * ((x + d) % 4) + core, tp) for d in (1, 3, 2)]
+    rights = [(8 * z_hi + 2 * ((x + d) % 4) + core, tp) for d in (1, 3)]
     twin = (ctx + sign, tp)
 
     quads = []
@@ -111,21 +110,24 @@
         to_z = (z + dz * sign + 4) % 4
         quads.append((to_z // 2) * 4 + (x + dx * sign + 4) % 4)
 
-    arrays = []
+    def boxes(begin, count):
+        columns = pl.ds(128 * begin, 128 * count)
+        return (
+            weight.at[7, pl.ds(0, 512), columns], weight.at[7, pl.ds(512, 512), columns],
+            work.at[pl.ds(TAPS + begin, count)],
+        )
+
     for step, q in enumerate(quads):
         columns = pl.ds(pl.multiple_of(q * 128, 128), 128)
-        copies = [
-            pltpu.make_async_copy(
-                inner_hbm.at[:, columns], weight.at[7, pl.ds(0, 512), pl.ds(128 * step, 128)], in_sem.at[step, 0]
-            ),
-            pltpu.make_async_copy(
-                signal_hbm.at[:, columns], weight.at[7, pl.ds(512, 512), pl.ds(128 * step, 128)], in_sem.at[step, 1]
-            ),
-            pltpu.make_async_copy(taps_hbm.at[:, columns], work.at[TAPS + step], in_sem.at[step, 2]),
-        ]
-        for copy in copies:
-            copy.start()
-        arrays.append(copies)
+        near, far, last = boxes(step, 1)
+        for i, (src, dst) in enumerate(((inner_hbm, near), (signal_hbm, far), (taps_hbm, last.at[0]))):
+            pltpu.make_async_copy(src.at[:, columns], dst, in_sem.at[min(step, 1), i]).start()
+
+    def landed(ref, sem):
+        pltpu.make_async_remote_copy(ref, ref, sem, sem, device_id=twin, device_id_type=MESH).wait_recv()
+
+    def departed(ref, sem):
+        pltpu.make_async_remote_copy(ref, ref, sem, sem, device_id=twin, device_id_type=MESH).wait_send()
 
     barrier = pltpu.get_barrier_semaphore()
     for q in quads:
@@ -158,11 +160,11 @@
     lane = lax.broadcasted_iota(jnp.int32, (128, 128), 1)
     first = lane < 64
     row0 = lax.broadcasted_iota(jnp.int32, (128, 128), 0)
-    sends = []
     for step, q in enumerate(quads):
         skip = skip_ref[:, pl.ds(pl.multiple_of(q * 128, 128), 128)]
-        for copy in arrays[step]:
-            copy.wait()
+        if step < 2:
+            for i, box in enumerate(boxes(step, 1 + 6 * step)):
+                pltpu.make_async_copy(box, box, in_sem.at[step, i]).wait()
 
         def pack(i, carry, step=step, skip=skip, q=q):
             start = pl.multiple_of(i * 128, 128)
@@ -176,76 +178,67 @@
 
         lax.fori_loop(0, 4, pack, 0)
         if step == 0:
-            pl.semaphore_wait(barrier, 22)
+            pl.semaphore_wait(barrier, 21)
         for dk in (0, 1):
             k = (core + dk) % 2
             copy = pltpu.make_async_remote_copy(
                 work.at[SEND + 2 * q + k], work.at[RECV + ctx],
-                out_send.at[2 * step + dk], out_recv.at[2 * step + dk],
+                out_send, out_recv,
                 device_id=(2 * q + k, partner_tp), device_id_type=MESH,
             )
             copy.start()
-            sends.append(copy)
     weights.append(load_weight(7))
     for copy in loads:
         copy.wait()
-    mine = [pl.multiple_of(256 * ((x + d) % 4) + 128 * core + 64 * z_hi, 64) for d in (0, 2)]
+    mine = pl.multiple_of(256 * x + 128 * core + 64 * z_hi, 64)
     for i in range(4):
         weights[i].wait()
     for u, (r, half) in enumerate(UNITS):
         for c in range(4):
             columns = slice(512 * half + 128 * c, 512 * half + 128 * c + 128)
-            for p in (0, 1):
-                share[u, p, c] = weight[SLOT[r], pl.ds(mine[p], 64), columns].astype(F32)
-    for copy in sends:
-        copy.wait_recv()
-
-    started = []
+            share[u, c] = weight[SLOT[r], pl.ds(mine, 64), columns].astype(F32)
+    landed(work.at[pl.ds(RECV, 16)], out_recv)
 
     def remote(src, dst, send_sem, recv_sem, device):
-        copy = pltpu.make_async_remote_copy(
+        pltpu.make_async_remote_copy(
             src, dst, send_sem, recv_sem, device_id=device, device_id_type=MESH
-        )
-        copy.start()
-        started.append(copy)
-        return copy
-
-    wz, wx, wc = {}, {}, {}
+        ).start()
 
     def give_z(u):
-        for p in range(1 + BY_Z[u]):
-            for h in (0, 1):
-                wz[u, p, h] = remote(
-                    share.at[u, p], wide.at[u, :, pl.ds(mine[p], 64)],
-                    wz_send.at[u, 2 * p + h], wz_recv.at[u, 2 * p + h], sides[h],
-                )
-
-    def quarter(u, d):
-        return wide.at[u, :, pl.ds(pl.multiple_of(256 * ((x + d) % 4) + 128 * core, 128), 128)]
+        for h in (0, 1):
+            remote(share.at[u], wide.at[u, :, pl.ds(mine, 64)], wz_send.at[u], wz_recv.at[u], sides[h])
+
+    def quarter(u, d, begin=0, count=128):
+        start = pl.multiple_of(256 * ((x + d) % 4) + 128 * core + begin, 64)
+        return wide.at[u, :, pl.ds(start, count)]
+
+    def rows_of_unit(u, count):
+        return wide.at[u, :, pl.ds(0, count)]
 
     def give_core(u, d):
-        wc[u, d] = remote(quarter(u, d), quarter(u, d), wc_send.at[u, d], wc_recv.at[u, d], twin)
+        remote(quarter(u, d), quarter(u, d), wc_send.at[u], wc_recv.at[u], twin)
 
     def spread(u):
-        for h in (0, 1):
-            wz[u, 0, h].wait_recv()
-        for n in range(3 - BY_Z[u]):
-            wx[u, n] = remote(quarter(u, 0), quarter(u, 0), wx_send.at[u, n], wx_recv.at[u, n], rights[n])
+        landed(quarter(u, 0), wz_recv.at[u])
+        for n in range(2):
+            remote(quarter(u, 0), quarter(u, 0), wx_send.at[u], wx_recv.at[u, 0], rights[n])
         give_core(u, 0)
-        if BY_Z[u]:
-            for h in (0, 1):
-                wz[u, 1, h].wait_recv()
-            give_core(u, 2)
 
     def pair_up(u):
-        for n, d in enumerate((3, 1) if BY_Z[u] else (3, 1, 2)):
-            wx[u, n].wait_recv()
+        landed(rows_of_unit(u, 256), wx_recv.at[u, 0])
+        for n, d in enumerate((3, 1)):
+            half = quarter(u, d, 64 * n, 64)
+            remote(half, half, wx_send.at[u], wx_recv.at[u, 1], rights[n])
+        for d in (3, 1):
             give_core(u, d)
 
+    def close(u):
+        landed(quarter(u, 2), wx_recv.at[u, 1])
+        give_core(u, 2)
+
     def fetch(u):
-        for n in range(4):
-            wc[u, n].wait_recv()
-        copy = pltpu.make_async_copy(wide.at[u], (result, home)[u % 2], wide_sem.at[u])
+        landed(rows_of_unit(u, 512), wc_recv.at[u])
+        copy = pltpu.make_async_copy(wide.at[u], (result, home)[u % 2], wide_sem.at[u % 2])
         copy.start()
         return copy
 
@@ -263,7 +256,7 @@
 
         lax.fori_loop(0, 8, convert, 0)
 
-    for u in range(5):
+    for u in range(4):
         give_z(u)
 
     first8 = lax.broadcasted_iota(jnp.int32, (8, 128), 1) < 64
@@ -276,7 +269,7 @@
         start = (pair % 2) * 256 + part * 128 + rows
         return work[PROD + pair // 2, pl.ds(pl.multiple_of(start, 8), 8), :]
 
-    def stage_one(a, carry):
+    def stage_one(a):
         parts = []
         for half in (0, 1):
             start = pl.multiple_of(half * 64 + a * 8, 8)
@@ -309,9 +302,9 @@
                 imag = out[16 * k1 + 8 : 16 * k1 + 16, half * 128 : half * 128 + 128]
                 put_spec(k1, 0, half, a, real * cos + imag * sin)
                 put_spec(k1, 1, half, a, imag * cos - real * sin)
-        return carry
-
-    lax.fori_loop(0, 8, stage_one, 0)
+
+    for a in range(8):
+        stage_one(a)
 
     def product(out, j):
         real, imag = out[:128, 128 * j : 128 * j + 128], out[128:, 128 * j : 128 * j + 128]
@@ -320,7 +313,7 @@
 
     first256 = lax.broadcasted_iota(jnp.int32, (256, 128), 1) < 64
 
-    def stage_two(i, carry):
+    def stage_two(i):
         value = jnp.concatenate([work[SPEC + 2 * i + j // 2, 256 * (j % 2) : 256 * (j % 2) + 256, :] for j in range(4)], axis=1)
         out = dot3(fwd_ref, value)
         pairs = [
@@ -329,16 +322,16 @@
         out = dot3(inv_ref, jnp.concatenate(pairs, axis=1))
         for j in range(2):
             work[PROD + i, 256 * j : 256 * j + 256, :] = out[:, 128 * j : 128 * j + 128]
-        return carry
-
-    lax.fori_loop(0, 4, stage_two, 0)
+
+    for i in range(4):
+        stage_two(i)
     spread(0)
-    lax.fori_loop(4, 8, stage_two, 0)
-    spread(1)
+    for i in range(4, 8):
+        stage_two(i)
     out = dot3(fwd_ref, work[SPEC + 16, 0:256, :])
     work[PROD + 8, 0:256, :] = dot3(inv_ref, product(out, 0))
 
-    def stage_three(a2, carry):
+    def stage_three(a2):
         sides = []
         for side in (0, 1):
             a = 2 * a2 + side
@@ -379,13 +372,11 @@
             value = out[:, 128 * side : 128 * side + 128].reshape(4, 16, 8, 128)
             for s in range(16):
                 result[:, pl.ds(pl.multiple_of(64 * s + (2 * a2 + side) * 8, 8), 8), :] = value[:, s]
-        return carry
-
-    lax.fori_loop(0, 4, stage_three, 0)
-
-    for copy in sends:
-        copy.wait_send()
-    returns = [[], [], [], []]
+
+    for a2 in range(4):
+        stage_three(a2)
+
+    departed(work.at[pl.ds(SEND, 16)], out_send)
 
     def give_back(part):
         for step, q in enumerate(quads):
@@ -394,20 +385,19 @@
                 copy = pltpu.make_async_remote_copy(
                     result.at[part, pl.ds(pl.multiple_of(64 * other, 64), 64)],
                     home.at[part, pl.ds(pl.multiple_of(64 * ctx, 64), 64)],
-                    back_send.at[part, 2 * step + dk], back_recv.at[part, 2 * step + dk],
+                    back_send.at[part], back_recv.at[part],
                     device_id=(other, partner_tp), device_id_type=MESH,
                 )
                 copy.start()
-                returns[part].append(copy)
 
     def receive(part):
-        for copy in returns[part]:
-            copy.wait_recv()
+        landed(home.at[part], back_recv.at[part])
 
     give_back(0)
     give_back(1)
     receive(0)
     give_back(2)
+    spread(1)
     first64 = lax.broadcasted_iota(jnp.int32, (64, 128), 1) < 64
 
     def gate(j, carry, keep=True):
@@ -426,7 +416,6 @@
                     give[j - 1, pl.ds(begin, 64), 128 * q : 128 * q + 128] = rounded.astype(F32)
         return carry
 
-    arrive = {}
     lane_of = {("b", 0): 0, ("b", 1): 1, ("a1", 1): 2, ("a2", 1): 3, ("a3", 1): 4}
 
     def rows_of(name):
@@ -444,9 +433,9 @@
         half = direction if m in (0, 2) else 1 - direction
         slot = 2 * m + direction
         at = lane_of[name, w]
-        arrive[name, w, m, direction] = remote(
+        remote(
             work.at[slots(r, w, half), rows_of(name), :], inbox(name, w, slot),
-            y_send.at[at, slot], y_recv.at[at, slot], up if direction == 0 else down,
+            y_send.at[at], y_recv.at[at, min(slot, 2)], up if direction == 0 else down,
         )
 
     def own(name, i):
@@ -485,8 +474,8 @@
             work[block + 2 * j + 1, rows, :] = work[block + 2 * j + 1, rows, :] + value[:, 128:]
 
     def accept(name):
-        arrive["z", name].wait_recv()
         at = AS.index(name)
+        landed(take.at[at], z_recv.at[at])
         other_mixed[128 * at : 128 * at + 128, :] = take[at].astype(BF16)
 
     def add(target, name, source):
@@ -495,14 +484,17 @@
 
     def pass_on(name, w, directions=(0, 1)):
         for direction in directions:
-            arrive[name, w, 0, direction].wait_recv()
+            landed(inbox(name, w, direction), y_recv.at[lane_of[name, w], direction])
             add(slots((1, 3)[direction], w, direction), name, inbox(name, w, direction))
             ring(name, w, 2, direction)
 
+    def box_of(name, w):
+        return in_b.at[w] if name == "b" else in_a.at[AS.index(name)]
+
     def gather(name, w):
+        landed(box_of(name, w).at[pl.ds(2, 4)], y_recv.at[lane_of[name, w], 2])
         for m in (1, 2):
             for direction in (0, 1):
-                arrive[name, w, m, direction].wait_recv()
                 half = direction if m == 2 else 1 - direction
                 add(slots(0, w, half), name, inbox(name, w, 2 * m + direction))
 
@@ -523,7 +515,7 @@
 
     def offer(at):
         gate(at + 1, 0)
-        arrive["z", AS[at]] = remote(give.at[at], take.at[at], z_send.at[at], z_recv.at[at], across)
+        remote(give.at[at], take.at[at], z_send.at[0], z_recv.at[at], across)
 
     for i in range(8):
         if i > 3:
@@ -534,28 +526,30 @@
             receive(1)
             give_back(3)
             offer(0)
+            give_z(4)
     pair_up(0)
-    pair_up(1)
     pass_on("b", 0)
     receive(2)
     offer(1)
+    give_z(5)
     spread(2)
+    pair_up(1)
     receive(3)
     spread(3)
     offer(2)
-    spread(4)
-    give_z(5)
+    pass_on("b", 1)
     give_z(6)
     give_z(7)
-    for part in returns:
-        for copy in part:
-            copy.wait_send()
-    first0, first1 = fetch(0), fetch(1)
-    for i in range(4, 8):
-        multiply(i, 128, 384)
-    pass_on("b", 1)
+    for part in range(4):
+        departed(result.at[part], back_send.at[part])
+    multiply(4, 128, 384)
+    close(0)
+    multiply(5, 128, 384)
+    close(1)
+    first0 = fetch(0)
+    multiply(6, 128, 384)
+    pair_up(2)
     settle(0, first0)
-    settle(1, first1)
 
     def first_step(name):
         accept(name)
@@ -564,53 +558,70 @@
         complete(1, [name])
         ring(name, 1, 0, 1)
 
-    first_step("a1")
-    pair_up(2)
+    accept("a1")
+    complete(0, ["a1"])
+    ring("a1", 1, 0, 0)
+    first1 = fetch(1)
+    multiply(7, 128, 384)
+    settle(1, first1)
+    complete(1, ["a1"])
+    ring("a1", 1, 0, 1)
+    pair_up(3)
+    spread(4)
+    first_step("a2")
+    close(2)
     settle(2, fetch(2))
-    complete(2, ["a1"])
+    complete(2, ["a1", "a2"])
     ring("a1", 1, 1, 0)
+    ring("a2", 1, 1, 0)
     gather("b", 0)
-    last = remote(work.at[slots(0, 0), rows_of("b"), :], in_zb, z_send.at[3], z_recv.at[3], across)
-    first_step("a2")
-    complete(2, ["a2"])
-    ring("a2", 1, 1, 0)
-    pair_up(3)
+    remote(work.at[slots(0, 0), rows_of("b"), :], in_zb, z_send.at[1], z_recv.at[3], across)
+    spread(5)
+    close(3)
     settle(3, fetch(3))
     complete(3, ["a1", "a2"])
     ring("a1", 1, 1, 1)
     ring("a2", 1, 1, 1)
+    pair_up(4)
     first_step("a3")
     complete(2, ["a3"])
     ring("a3", 1, 1, 0)
     complete(3, ["a3"])
     ring("a3", 1, 1, 1)
-    spread(5)
-    pair_up(4)
+    close(4)
+    pair_up(5)
     settle(4, fetch(4))
     complete(4, AS)
-    for name in AS:
+    spread(6)
+    for name in AS[:2]:
         pass_on(name, 1, (0,))
-    spread(6)
-    pair_up(5)
+    close(5)
     settle(5, fetch(5))
     complete(5, AS)
-    for name in AS:
+    spread(7)
+    for name in AS[:2]:
         pass_on(name, 1, (1,))
-    spread(7)
     pair_up(6)
+    pass_on("a3", 1)
     pair_up(7)
     gather("b", 1)
-    last.wait_recv()
+    landed(in_zb, z_recv.at[3])
     finish("b", in_zb)
-    settle(6, fetch(6))
-    complete(6, AS)
-    settle(7, fetch(7))
-    complete(7, AS)
+    for u in (6, 7):
+        close(u)
+        settle(u, fetch(u))
+        complete(u, AS)
     for name in AS:
         gather(name, 1)
         finish(name)
-    for copy in started:
-        copy.wait_send()
+    for u in range(8):
+        departed(rows_of_unit(u, 128), wz_send.at[u])
+        departed(rows_of_unit(u, 384), wx_send.at[u])
+        departed(rows_of_unit(u, 512), wc_send.at[u])
+    for (name, w), at in lane_of.items():
+        departed(box_of(name, w), y_send.at[at])
+    departed(give, z_send.at[0])
+    departed(in_zb, z_send.at[1])
     for copy in writes:
         copy.wait()
 
@@ -647,11 +658,11 @@
             pltpu.VMEM((3, 128, 1024), F32),
             pltpu.VMEM((3, 128, 1024), F32),
             pltpu.VMEM((384, 1024), BF16),
-            pltpu.VMEM((8, 2, 4, 64, 128), F32),
-            dma((8, 3)), dma((6,)), dma((8,)), dma((8,)), dma((4,)),
-            dma((16,)), dma((16,)), dma((4, 16)), dma((4, 16)),
-            dma((5, 6)), dma((5, 6)), dma((4,)), dma((4,)),
-            dma((8, 4)), dma((8, 4)), dma((8, 3)), dma((8, 3)), dma((8, 4)), dma((8, 4)),
+            pltpu.VMEM((8, 4, 64, 128), F32),
+            dma((2, 3)), dma((6,)), dma((8,)), dma((2,)), dma((4,)),
+            dma, dma, dma((4,)), dma((4,)),
+            dma((5,)), dma((5, 3)), dma((2,)), dma((4,)),
+            dma((8,)), dma((8,)), dma((8,)), dma((8, 2)), dma((8,)), dma((8,)),
         ],
         compiler_params=pltpu.CompilerParams(
             collective_id=0, has_side_effects=True, vmem_limit_bytes=62 << 20

time: 183 us -> 174 us (0.951)
  Pallas kernels: 181 us -> 172 us
    pallas_call x1, Pallas kernels: 181 us -> 172 us  [shards(): pl.pallas_call(layer_kernel, name='layer', out_shape=(jax.ShapeDtypeStruc...]
where the time goes in v4:
time: 174 us
  Pallas kernels  172 us (99%)
  local copies, waits for them, and re-layouts  2.26 us (1%)
    pallas_call x1, Pallas kernels, shards(): pl.pallas_call(layer_kernel, name='layer', out_shape=(jax.ShapeDtypeStruc...  172 us

profile of v4, /device:TPU:1, one launch (start us, length us, event | category | flops | bytes accessed | tf_op | source)
XLA Modules:
  0.0 174.1 jit_solution(9581179862290558933)
XLA Ops:
  0.0 171.8 %layer.1 = (bf16[512,1024]{1,0:T(8,128)(2,1)}, f32[8,4,1024,128]{3,2,1,0:T(8,128)}) custom-call(f32[1,1024]{1,0:T(1,128)} %bitcast.1, bf16[512,1024]{1,0:T(8,128)(2,1)} %inner_hbm.1, bf16[512,1024]{1,0:T(8,128)(2,1)} %signal_hbm.1, f32[512,1024]{1,0:T(8,128)} %taps_hbm.1, bf16[512,1024]{1,0:T(8,128)(2,1)} %outer_hbm.1, bf16[1024,8192]{1,0:T(8,128)(2,1)} %weight_hbm.1, ...), custom_call_target="tpu_custom_call" | custom-call | tf_op jit(solution)/shard_map/layer/pallas_call | solution.py:633
  171.8 2.3 %copy.13 = bf16[512,1024]{1,0:T(8,128)(2,1)} copy(bf16[512,1024]{1,0:T(8,128)(2,1)} %get-tuple-element.6) | data formatting | bytes 2097152

commit v5 on v4

--- a/solution.py
+++ b/solution.py
@@ -397,7 +397,6 @@
     give_back(1)
     receive(0)
     give_back(2)
-    spread(1)
     first64 = lax.broadcasted_iota(jnp.int32, (64, 128), 1) < 64
 
     def gate(j, carry, keep=True):
@@ -526,29 +525,28 @@
             receive(1)
             give_back(3)
             offer(0)
-            give_z(4)
-    pair_up(0)
+            pair_up(0)
+            spread(1)
     pass_on("b", 0)
     receive(2)
     offer(1)
+    give_z(4)
     give_z(5)
     spread(2)
-    pair_up(1)
     receive(3)
-    spread(3)
     offer(2)
-    pass_on("b", 1)
     give_z(6)
     give_z(7)
     for part in range(4):
         departed(result.at[part], back_send.at[part])
     multiply(4, 128, 384)
     close(0)
+    first0 = fetch(0)
     multiply(5, 128, 384)
-    close(1)
-    first0 = fetch(0)
+    pass_on("b", 1)
+    pair_up(1)
+    spread(3)
     multiply(6, 128, 384)
-    pair_up(2)
     settle(0, first0)
 
     def first_step(name):
@@ -561,14 +559,16 @@
     accept("a1")
     complete(0, ["a1"])
     ring("a1", 1, 0, 0)
+    pair_up(2)
+    close(1)
     first1 = fetch(1)
     multiply(7, 128, 384)
     settle(1, first1)
     complete(1, ["a1"])
     ring("a1", 1, 0, 1)
     pair_up(3)
+    first_step("a2")
     spread(4)
-    first_step("a2")
     close(2)
     settle(2, fetch(2))
     complete(2, ["a1", "a2"])

time: 174 us -> 174 us (level)
  no operation moved by 1% of the time
where the time goes in v5:
time: 174 us
  Pallas kernels  171 us (98%)
  local copies, waits for them, and re-layouts  2.26 us (1%)
    pallas_call x1, Pallas kernels, shards(): pl.pallas_call(layer_kernel, name='layer', out_shape=(jax.ShapeDtypeStruc...  171 us

profile of v5, /device:TPU:1, one launch (start us, length us, event | category | flops | bytes accessed | tf_op | source)
XLA Modules:
  0.0 173.7 jit_solution(9921156762870647184)
XLA Ops:
  0.0 171.4 %layer.1 = (bf16[512,1024]{1,0:T(8,128)(2,1)}, f32[8,4,1024,128]{3,2,1,0:T(8,128)}) custom-call(f32[1,1024]{1,0:T(1,128)} %bitcast.1, bf16[512,1024]{1,0:T(8,128)(2,1)} %inner_hbm.1, bf16[512,1024]{1,0:T(8,128)(2,1)} %signal_hbm.1, f32[512,1024]{1,0:T(8,128)} %taps_hbm.1, bf16[512,1024]{1,0:T(8,128)(2,1)} %outer_hbm.1, bf16[1024,8192]{1,0:T(8,128)(2,1)} %weight_hbm.1, ...), custom_call_target="tpu_custom_call" | custom-call | tf_op jit(solution)/shard_map/layer/pallas_call | solution.py:633
  171.4 2.3 %copy.13 = bf16[512,1024]{1,0:T(8,128)(2,1)} copy(bf16[512,1024]{1,0:T(8,128)(2,1)} %get-tuple-element.6) | data formatting | bytes 2097152
